TPU v7x, 32 devices: a whole 2x2x4 slice. The times are simulated.
32 devices in a mesh: lat: 4 (over z), lon: 8 (over y, x, core).
Axes of the slice: x: 2, y: 2, z: 4, core: 2. Of those that a mesh axis runs over, the one named last changes fastest.
Arguments:
- winds: float32 [2, 256, 23040], P(None, 'lat', 'lon'), may hold values from -6 to 6
- thickness: float32 [256, 23040], P('lat', 'lon'), may hold values from 0.5 to 1.5
- tracer: float32 [256, 23040], P('lat', 'lon'), may hold values from -6 to 6
- cutoff: int32 [256], P('lat'), may hold values from 1 to 1440, as said below
- damping: float32 [256], P('lat'), may hold values from 0.2 to 1
Outputs:
- new_winds: float32 [2, 256, 23040], P(None, 'lat', 'lon')
- new_thickness: float32 [256, 23040], P('lat', 'lon')
- new_tracer: float32 [256, 23040], P('lat', 'lon')
Inputs may be any that keep to these rules, and one draw needn't show every extreme that they name: cutoff is a wavenumber of 1 to 1440.
All inputs are finite; a program needn't handle non-finite values.
Results may differ from a plain program's by a relative error of at most 0.0003.
Values sent between devices are 32-bit elements; how exact they have to be, the bound alone decides.
A program may use at most 128 MiB of HBM per device.

v0:
```python
import math

import jax
import jax.numpy as jnp
from jax import lax
from jax.sharding import PartitionSpec as P

LEV = 8


def from_partner(block, axis, stride):
    count = lax.axis_size(axis)
    route = []
    for low in range(count):
        high = low | 1 << stride
        if high != low and high < count:
            route += [(low, high), (high, low)]
    return lax.ppermute(block, axis, route)


def extended(block, sides, width, periodic):
    for axis, dim in sides:
        count = lax.axis_size(axis)
        forward = [(i, i + 1) for i in range(count - 1)]
        if periodic:
            forward.append((count - 1, 0))
        backward = [(target, source) for source, target in forward]
        low = lax.ppermute(
            lax.slice_in_dim(block, block.shape[dim] - width, None, axis=dim), axis, forward
        )
        high = lax.ppermute(lax.slice_in_dim(block, 0, width, axis=dim), axis, backward)
        block = jnp.concatenate([low, block, high], axis=dim)
    return block


def transform(values, cutoffs, damping):
    row_total = values.shape[0]
    length = values.shape[1] // LEV
    shaped = values.reshape(row_total, length, LEV)
    modes = length // 2 + 1
    block_size = min(512, modes)
    positions = jnp.arange(length, dtype=jnp.int32)
    result = shaped
    for start in range(0, modes, block_size):
        wavenumber = start + jnp.arange(block_size, dtype=jnp.int32)
        phases = (positions[:, None] * wavenumber[None, :] % length).astype(jnp.float32) * (
            2.0 * math.pi / length
        )
        cosines = jnp.cos(phases)
        sines = jnp.sin(phases)
        wave_float = wavenumber.astype(jnp.float32)
        mode_scale = jnp.where(
            (wavenumber == 0) | (wavenumber * 2 == length), 1.0 / length, 2.0 / length
        )
        ratios = cutoffs[:, None] / jnp.maximum(wave_float, 1.0)[None, :]
        active = (wavenumber[None, :] < modes) & (wave_float[None, :] > cutoffs[:, None])
        weights = jnp.where(
            active, (1.0 - damping[:, None] * ratios * ratios) * mode_scale[None, :], 0.0
        )
        cos_part = jnp.einsum("rnl,nk->rlk", shaped, cosines, precision=lax.Precision.HIGHEST)
        sin_part = jnp.einsum("rnl,nk->rlk", shaped, sines, precision=lax.Precision.HIGHEST)
        result = result - jnp.einsum(
            "rlk,nk->rnl", cos_part * weights[:, None, :], cosines, precision=lax.Precision.HIGHEST
        )
        result = result - jnp.einsum(
            "rlk,nk->rnl", sin_part * weights[:, None, :], sines, precision=lax.Precision.HIGHEST
        )
    return result.reshape(row_total, length * LEV)


def filter_band(flat_rows, row_params):
    owned_rows = lax.all_to_all(flat_rows, "lon", split_axis=0, concat_axis=1, tiled=True)
    owned = owned_rows.shape[0]
    lat_count = row_params.shape[1]
    owner_index = lax.axis_index("lon")
    flat_index = owner_index * owned + jnp.arange(owned, dtype=jnp.int32)
    local_lat = flat_index % lat_count
    select = (local_lat[:, None] == jnp.arange(lat_count, dtype=jnp.int32)[None, :]).astype(
        jnp.float32
    )
    cutoffs = jnp.sum(select * row_params[0][None, :], axis=1)
    damping = jnp.sum(select * row_params[1][None, :], axis=1)
    filtered = transform(owned_rows, cutoffs, damping)
    return lax.all_to_all(filtered, "lon", split_axis=1, concat_axis=0, tiled=True)


def per_device(winds, thickness, tracer, cutoff, damping):
    lat_size = lax.axis_size("lat")
    lon_size = lax.axis_size("lon")
    band_index = lax.axis_index("lat")
    row_count, width = thickness.shape
    columns = width // LEV
    nlon_total = columns * lon_size
    nlat_total = row_count * lat_size
    fields = jnp.concatenate([winds, thickness[None], tracer[None]], axis=0)
    flat_rows = fields.reshape(4 * row_count, width)
    is_polar = (band_index < lat_size // 4) | (band_index >= lat_size - lat_size // 4)
    row_params = jnp.stack([cutoff.astype(jnp.float32), damping])
    half_rows = flat_rows.shape[0] // 2
    partner_bit = lat_size.bit_length() - 3
    lent_rows, lent_params = from_partner((flat_rows[half_rows:], row_params), "lat", partner_bit)
    work_rows = jnp.where(is_polar, flat_rows[:half_rows], lent_rows)
    work_params = jnp.where(is_polar, row_params, lent_params)
    done_rows = filter_band(work_rows, work_params)
    returned = from_partner(done_rows, "lat", partner_bit)
    filtered = jnp.where(is_polar, jnp.concatenate([done_rows, returned], axis=0), flat_rows)
    filtered = filtered.reshape(4, row_count, width)
    zonal = filtered[0]
    meridional = filtered[1]
    layer = filtered[2]
    tracer_mass = filtered[3]
    edge_pair = jnp.stack([layer[0], layer[-1]])
    partner_edges = from_partner(edge_pair, "lon", lon_size.bit_length() - 2)
    padded = extended(jnp.stack([meridional, layer, tracer_mass]), (("lat", 1),), 1, False)
    south_rim = jnp.where(band_index == 0, partner_edges[0], padded[1][0])
    north_rim = jnp.where(band_index == lat_size - 1, partner_edges[1], padded[1][-1])
    wind_pad = padded[0]
    layer_pad = jnp.concatenate([south_rim[None], padded[1][1:-1], north_rim[None]], axis=0)
    tracer_pad = padded[2]
    sides = extended(jnp.stack([zonal, layer, tracer_mass]), (("lon", 2),), LEV, True)
    lon_step = 2.0 * math.pi / nlon_total
    lat_step = math.pi / nlat_total
    global_rows = (band_index * row_count + jnp.arange(row_count, dtype=jnp.int32)).astype(
        jnp.float32
    )
    cos_center = jnp.cos(-math.pi / 2 + (global_rows + 0.5) * lat_step)[:, None]
    face_index = band_index * row_count + jnp.arange(row_count + 1, dtype=jnp.int32)
    face_float = face_index.astype(jnp.float32)
    cos_face = jnp.where(
        (face_index == 0) | (face_index == nlat_total),
        0.0,
        jnp.cos(-math.pi / 2 + face_float * lat_step),
    )[:, None]
    reach = 2 * LEV
    zonal_east = sides[0][:, reach:]
    zonal_west = sides[0][:, :-reach]
    layer_east = sides[1][:, reach:]
    layer_west = sides[1][:, :-reach]
    tracer_east_cell = sides[2][:, reach:]
    tracer_west_cell = sides[2][:, :-reach]
    flux_east = 0.25 * (zonal + zonal_east) * (layer + layer_east)
    flux_west = 0.25 * (zonal_west + zonal) * (layer_west + layer)
    tracer_east = 0.25 * (zonal + zonal_east) * (tracer_mass + tracer_east_cell)
    tracer_west = 0.25 * (zonal_west + zonal) * (tracer_west_cell + tracer_mass)
    wind_face = wind_pad[:-1] + wind_pad[1:]
    flux_north = 0.25 * wind_face * (layer_pad[:-1] + layer_pad[1:]) * cos_face
    tracer_north = 0.25 * wind_face * (tracer_pad[:-1] + tracer_pad[1:]) * cos_face
    layer_div = (
        (flux_east - flux_west) / lon_step + (flux_north[1:] - flux_north[:-1]) / lat_step
    ) / cos_center
    tracer_div = (
        (tracer_east - tracer_west) / lon_step + (tracer_north[1:] - tracer_north[:-1]) / lat_step
    ) / cos_center
    new_layer = layer - lon_step * layer_div
    new_tracer = tracer_mass - lon_step * tracer_div
    new_zonal = zonal - lon_step * (layer_east - layer_west) / (2.0 * lon_step * cos_center)
    new_meridional = meridional - lon_step * (layer_pad[2:] - layer_pad[:-2]) / (2.0 * lat_step)
    return (jnp.stack([new_zonal, new_meridional]), new_layer, new_tracer)


def solution(mesh):
    placed = (P(None, "lat", "lon"), P("lat", "lon"), P("lat", "lon"), P("lat"), P("lat"))
    return jax.shard_map(
        per_device,
        mesh=mesh,
        in_specs=placed,
        out_specs=(P(None, "lat", "lon"), P("lat", "lon"), P("lat", "lon")),
        check_vma=False,
    )
```

profile of v0, /device:TPU:0, one launch (start us, length us, event | category | flops | bytes accessed | tf_op | source)
XLA Modules:
  0.0 518.8 jit_solution(1144758493805503672)
XLA Ops:
  7.0 32.4 %collective-permute-done = f32[128,2880]{0,1:T(8,128)} collective-permute-done((f32[128,2880]{0,1:T(8,128)}, f32[128,2880]{0,1:T(8,128)}, u32[]{:S(2)}, u32[]{:S(2)}) %collective-permute-start) | collective-permute-done | bytes 1474592 | tf_op jit(solution)/shard_map/ppermute | solution.py:18
  42.5 3.9 all-to-all-start
  46.8 19.9 %all-to-all-done = f32[8,16,2880]{2,1,0:T(8,128)S(1)} async-done(((f32[8,16,2880]{2,1,0:T(8,128)}), f32[8,16,2880]{2,1,0:T(8,128)S(1)}, u32[]{:S(2)}, u32[]{:S(2)}) %all-to-all-start) | async-done | bytes 1474592 | tf_op jit(solution)/shard_map/all_to_all | solution.py:72
  66.8 6.4 %copy.50 = f32[16,8,2880]{0,2,1:T(8,128)} copy(f32[16,8,2880]{2,0,1:T(8,128)S(1)} %bitcast.165) | data formatting | bytes 2949120 | tf_op jit(solution)/shard_map/all_to_all | solution.py:72
  73.2 7.1 %copy.52 = f32[16,2880,8]{1,0,2:T(8,128)S(1)} copy(f32[16,2880,8]{0,2,1:T(8,128)} %bitcast.161) | data formatting | bytes 2949120 | tf_op jit(solution)/shard_map/reshape | solution.py:39
  80.3 26.8 %fusion.152 = f32[16,8,512]{2,0,1:T(8,128)S(1)} fusion(f32[16,2880,8]{1,0,2:T(8,128)S(1)} %copy.52, s32[512]{0:T(512)S(1)} %iota_add_fusion, f32[16,512]{1,0:T(8,128)S(1)} %get-tuple-element.29), kind=kOutput, calls=%fused_computation.113 | convolution fusion | flops 2278260736 | bytes 1771520 | tf_op jit(solution)/shard_map/rnl,nk->rlk/dot_general | solution.py:61
  107.1 26.1 %fusion.149 = f32[16,8,512]{2,0,1:T(8,128)S(1)} fusion(f32[16,2880,8]{1,0,2:T(8,128)S(1)} %copy.52, s32[512]{0:T(512)S(1)} %iota_add_fusion, f32[16,512]{1,0:T(8,128)S(1)} %get-tuple-element.29), kind=kOutput, calls=%fused_computation.112 | convolution fusion | flops 2278260736 | bytes 1771520 | tf_op jit(solution)/shard_map/rnl,nk->rlk/dot_general | solution.py:60
  133.2 26.8 %fusion.146 = f32[16,8,512]{2,0,1:T(8,128)S(1)} fusion(f32[16,2880,8]{1,0,2:T(8,128)S(1)} %copy.52, s32[512]{0:T(512)S(1)} %iota_add_fusion.1, f32[16,512]{1,0:T(8,128)S(1)} %get-tuple-element.28), kind=kOutput, calls=%fused_computation.111 | convolution fusion | flops 2278260736 | bytes 1771520 | tf_op jit(solution)/shard_map/rnl,nk->rlk/dot_general | solution.py:61
  160.0 26.1 %fusion.143 = f32[16,8,512]{2,0,1:T(8,128)S(1)} fusion(f32[16,2880,8]{1,0,2:T(8,128)S(1)} %copy.52, s32[512]{0:T(512)S(1)} %iota_add_fusion.1, f32[16,512]{1,0:T(8,128)S(1)} %get-tuple-element.28), kind=kOutput, calls=%fused_computation.110 | convolution fusion | flops 2278260736 | bytes 1771520 | tf_op jit(solution)/shard_map/rnl,nk->rlk/dot_general | solution.py:60
  186.1 26.3 %fusion.137 = f32[16,8,512]{2,0,1:T(8,128)S(1)} fusion(f32[16,2880,8]{1,0,2:T(8,128)S(1)} %copy.52, f32[16,512]{1,0:T(8,128)S(1)} %get-tuple-element.27), kind=kOutput, calls=%fused_computation.108 | convolution fusion | flops 2278260736 | bytes 1769472 | tf_op jit(solution)/shard_map/rnl,nk->rlk/dot_general | solution.py:60
  212.4 26.7 %fusion.140 = f32[16,8,512]{2,0,1:T(8,128)S(1)} fusion(f32[16,2880,8]{1,0,2:T(8,128)S(1)} %copy.52, f32[16,512]{1,0:T(8,128)S(1)} %get-tuple-element.27), kind=kOutput, calls=%fused_computation.109 | convolution fusion | flops 2278260736 | bytes 1769472 | tf_op jit(solution)/shard_map/rnl,nk->rlk/dot_general | solution.py:61
  239.1 29.3 %fusion.66 = f32[16,2880,8]{1,0,2:T(8,128)S(1)} fusion(f32[16,8,512]{2,0,1:T(8,128)S(1)} %fusion.152, s32[512]{0:T(512)S(1)} %iota_add_fusion), kind=kOutput, calls=%fused_computation.54 | convolution fusion | flops 2278195200 | bytes 1738752 | tf_op jit(solution)/shard_map/rlk,nk->rnl/dot_general | solution.py:65
  268.4 28.5 %fusion.63 = f32[16,2880,8]{1,0,2:T(8,128)S(1)} fusion(f32[16,8,512]{2,0,1:T(8,128)S(1)} %fusion.149, s32[512]{0:T(512)S(1)} %iota_add_fusion), kind=kOutput, calls=%fused_computation.53 | convolution fusion | flops 2278195200 | bytes 1738752 | tf_op jit(solution)/shard_map/rlk,nk->rnl/dot_general | solution.py:62
  296.9 29.3 %fusion.60 = f32[16,2880,8]{1,0,2:T(8,128)S(1)} fusion(f32[16,8,512]{2,0,1:T(8,128)S(1)} %fusion.146, s32[512]{0:T(512)S(1)} %iota_add_fusion.1), kind=kOutput, calls=%fused_computation.52 | convolution fusion | flops 2278195200 | bytes 1738752 | tf_op jit(solution)/shard_map/rlk,nk->rnl/dot_general | solution.py:65
  326.2 28.5 %fusion.57 = f32[16,2880,8]{1,0,2:T(8,128)S(1)} fusion(f32[16,8,512]{2,0,1:T(8,128)S(1)} %fusion.143, s32[512]{0:T(512)S(1)} %iota_add_fusion.1), kind=kOutput, calls=%fused_computation.51 | convolution fusion | flops 2278195200 | bytes 1738752 | tf_op jit(solution)/shard_map/rlk,nk->rnl/dot_general | solution.py:62
  354.7 29.0 %fusion.81 = f32[16,2880,8]{1,0,2:T(8,128)S(1)} fusion(f32[16,2880,8]{1,0,2:T(8,128)S(1)} %copy.52, f32[16,8,512]{2,0,1:T(8,128)S(1)} %fusion.137), kind=kOutput, calls=%fused_computation.59 | convolution fusion | flops 2278563840 | bytes 3211264 | tf_op jit(solution)/shard_map/rlk,nk->rnl/dot_general | solution.py:62
  383.7 29.8 %fusion.90 = f32[16,2880,8]{1,0,2:T(8,128)S(1)} fusion(f32[16,2880,8]{1,0,2:T(8,128)S(1)} %fusion.66, f32[16,2880,8]{1,0,2:T(8,128)S(1)} %fusion.63, f32[16,2880,8]{1,0,2:T(8,128)S(1)} %fusion.60, f32[16,2880,8]{1,0,2:T(8,128)S(1)} %fusion.57, f32[16,2880,8]{1,0,2:T(8,128)S(1)} %fusion.81, f32[16,8,512]{2,0,1:T(8,128)S(1)} %fusion.140), kind=kOutput, calls=%fused_computation.62 | convolution fusion | flops 2280038400 | bytes 9109504 | tf_op jit(solution)/shard_map/rlk,nk->rnl/dot_general | solution.py:65
  413.5 6.5 %copy.58 = f32[16,2880,8]{0,2,1:T(8,128)} copy(f32[16,2880,8]{1,0,2:T(8,128)S(1)} %fusion.90) | data formatting | bytes 2949120 | tf_op jit(solution)/shard_map/sub | solution.py:65
  419.9 8.0 %copy.59 = f32[16,8,2880]{2,0,1:T(8,128)} copy(f32[16,8,2880]{0,2,1:T(8,128)} %bitcast.162) | data formatting | bytes 2949120 | tf_op jit(solution)/shard_map/all_to_all | solution.py:84
  428.0 23.8 %all_to_all.35 = f32[16,8,2880]{2,0,1:T(8,128)S(1)} all-to-all(f32[16,8,2880]{2,0,1:T(8,128)} %copy.59), channel_id=1, replica_groups=mesh['lat'=4,'lon'=8] {'lon'}, dimensions={1} | all-to-all | bytes 2949120 | tf_op jit(solution)/shard_map/all_to_all | solution.py:84
  455.1 3.2 pad_maximum_fusion
  458.2 29.2 %collective-permute-done.2 = f32[128,2880]{0,1:T(8,128)} collective-permute-done((f32[128,2880]{0,1:T(8,128)}, f32[128,2880]{0,1:T(8,128)}, u32[]{:S(2)}, u32[]{:S(2)}) %collective-permute-start.2) | collective-permute-done | bytes 1474592 | tf_op jit(solution)/shard_map/ppermute | solution.py:18
  501.9 4.5 collective-permute-start.7
  506.4 4.3 concatenate.33
  (76 shorter events, 35.3 us)
Async XLA Ops:
  0.6 6.2 %copy-start.11 = (s32[64]{0:T(128)S(1)}, s32[64]{0:T(128)}, u32[]{:S(2)}) copy-start(s32[64]{0:T(128)} %param.8) | copy-start | bytes 772
  0.6 6.2 %copy-start.10 = (f32[64]{0:T(128)S(1)}, f32[64]{0:T(128)}, u32[]{:S(2)}) copy-start(f32[64]{0:T(128)} %param.9) | copy-start | bytes 772
  0.7 40.6 %copy-start.9 = (f32[2,64,2880]{2,1,0:T(8,128)S(1)}, f32[2,64,2880]{2,1,0:T(8,128)}, u32[]{:S(2)}) copy-start(f32[2,64,2880]{2,1,0:T(8,128)} %param.5) | copy-start | bytes 4423684
  3.8 35.6 %collective-permute-start = (f32[128,2880]{0,1:T(8,128)}, f32[128,2880]{0,1:T(8,128)}, u32[]{:S(2)}, u32[]{:S(2)}) collective-permute-start(f32[128,2880]{0,1:T(8,128)} %copy.48), channel_id=1, source_target_pairs={{0,8},{8,0},{16,24},{24,16},{1,9},{9,1},{17,25},{25,17},{2,10},{10... | collective-permute-start | bytes 4423688 | tf_op jit(solution)/shard_map/ppermute | solution.py:18
  6.8 39.7 %collective-permute-start.1 = (f32[2,64]{1,0:T(2,128)S(1)}, f32[2,64]{1,0:T(2,128)S(1)}, u32[]{:S(2)}, u32[]{:S(2)}) collective-permute-start(f32[2,64]{1,0:T(2,128)S(1)} %pad_maximum_fusion.16), channel_id=1, source_target_pairs={{0,8},{8,0},{16,24},{24,16},{1,9},{9,1},{17,25},{25,17},{2,10},{10... | collective-permute-start | bytes 1544 | tf_op jit(solution)/shard_map/ppermute | solution.py:18
  42.5 24.2 %all-to-all-start = ((f32[8,16,2880]{2,1,0:T(8,128)}), f32[8,16,2880]{2,1,0:T(8,128)S(1)}, u32[]{:S(2)}, u32[]{:S(2)}) async-start(f32[8,16,2880]{2,1,0:T(8,128)} %bitcast.166), calls=%async_computation | async-start | bytes 3014656 | tf_op jit(solution)/shard_map/all_to_all | solution.py:72
  451.7 35.7 %copy-start = (f32[16,8,2880]{2,0,1:T(8,128)}, f32[16,8,2880]{2,0,1:T(8,128)S(1)}, u32[]{:S(2)}) copy-start(f32[16,8,2880]{2,0,1:T(8,128)S(1)} %all_to_all.35) | copy-start | bytes 4423684
  453.3 34.0 %collective-permute-start.2 = (f32[128,2880]{0,1:T(8,128)}, f32[128,2880]{0,1:T(8,128)}, u32[]{:S(2)}, u32[]{:S(2)}) collective-permute-start(f32[128,2880]{0,1:T(8,128)} %copy.60), channel_id=1, source_target_pairs={{0,8},{8,0},{16,24},{24,16},{1,9},{9,1},{17,25},{25,17},{2,10},{10... | collective-permute-start | bytes 4423688 | tf_op jit(solution)/shard_map/ppermute | solution.py:18
  494.6 0.9 copy-start.1
  494.6 1.2 copy-start.3
  494.6 1.4 copy-start.5
  495.8 1.4 copy-start.7
  497.2 9.2 %collective-permute-start.3 = (f32[3,64,8]{2,1,0:T(8,128)S(1)}, f32[3,64,8]{2,1,0:T(8,128)S(1)}, u32[]{:S(2)}, u32[]{:S(2)}) collective-permute-start(f32[3,64,8]{2,1,0:T(8,128)S(1)} %get-tuple-element.20), channel_id=1, source_target_pairs={{0,1},{1,2},{2,3},{3,4},{4,5},{5,6},{6,7},{7,0},{8,9},{9,10},{10,1... | collective-permute-start | bytes 18440 | tf_op jit(solution)/shard_map/ppermute | solution.py:28
  497.2 9.2 %collective-permute-start.4 = (f32[3,64,8]{2,1,0:T(8,128)S(1)}, f32[3,64,8]{2,1,0:T(8,128)S(1)}, u32[]{:S(2)}, u32[]{:S(2)}) collective-permute-start(f32[3,64,8]{2,1,0:T(8,128)S(1)} %get-tuple-element.19), channel_id=1, source_target_pairs={{1,0},{2,1},{3,2},{4,3},{5,4},{6,5},{7,6},{0,7},{9,8},{10,9},{11,1... | collective-permute-start | bytes 18440 | tf_op jit(solution)/shard_map/ppermute | solution.py:31
  499.9 12.7 %collective-permute-start.6 = (f32[3,1,2880]{2,1,0:T(1,128)S(1)}, f32[3,1,2880]{2,1,0:T(1,128)S(1)}, u32[]{:S(2)}, u32[]{:S(2)}) collective-permute-start(f32[3,1,2880]{2,1,0:T(1,128)S(1)} %get-tuple-element.21), channel_id=1, source_target_pairs={{8,0},{16,8},{24,16},{9,1},{17,9},{25,17},{10,2},{18,10},{26,18},{... | collective-permute-start | bytes 103688 | tf_op jit(solution)/shard_map/ppermute | solution.py:31
  501.3 11.4 %collective-permute-start.5 = (f32[2,2880]{1,0:T(2,128)S(1)}, f32[2,2880]{1,0:T(2,128)S(1)}, u32[]{:S(2)}, u32[]{:S(2)}) collective-permute-start(f32[2,2880]{1,0:T(2,128)S(1)} %pad_maximum_fusion.15), channel_id=1, source_target_pairs={{0,4},{4,0},{1,5},{5,1},{2,6},{6,2},{3,7},{7,3},{8,12},{12,8},{9,1... | collective-permute-start | bytes 69128 | tf_op jit(solution)/shard_map/ppermute | solution.py:18
  501.9 10.8 %collective-permute-start.7 = (f32[3,1,2880]{2,1,0:T(1,128)S(1)}, f32[3,1,2880]{2,1,0:T(1,128)S(1)}, u32[]{:S(2)}, u32[]{:S(2)}) collective-permute-start(f32[3,1,2880]{2,1,0:T(1,128)S(1)} %get-tuple-element.22), channel_id=1, source_target_pairs={{0,8},{8,16},{16,24},{1,9},{9,17},{17,25},{2,10},{10,18},{18,26},{... | collective-permute-start | bytes 103688 | tf_op jit(solution)/shard_map/ppermute | solution.py:28
  510.7 5.1 copy-start.2
  510.7 5.1 copy-start.4
  510.7 5.1 copy-start.6
  512.6 3.5 copy-start.8
where the time goes:
time: 527 us; the launch traced here: 519 us
  matrix products  333 us (63%)
  waiting for transfers between devices  81.6 us (15%)
  local copies, waits for them, and re-layouts  45.7 us (9%)
  blocking collectives  23.8 us (5%)
  starting transfers between devices  17.7 us (3%)
  other arithmetic  15.8 us (3%)
    dot_general x3, matrix products, transform(): jnp.einsum('rlk,nk->rnl', sin_part * weights[:, None, :], sines, precisio...  88.3 us
    dot_general x3, matrix products, transform(): jnp.einsum('rlk,nk->rnl', cos_part * weights[:, None, :], cosines, precis...  86 us
    dot_general x3, matrix products, transform(): jnp.einsum('rnl,nk->rlk', shaped, sines, precision=lax.Precision.HIGHEST)  80.3 us
    dot_general x3, matrix products, transform(): jnp.einsum('rnl,nk->rlk', shaped, cosines, precision=lax.Precision.HIGHEST)  78.4 us
    ppermute x4, waiting for transfers between devices, from_partner(): return lax.ppermute(block, axis, route)  61.6 us
    all_to_all x1, blocking collectives, filter_band(): lax.all_to_all(filtered, 'lon', split_axis=1, concat_axis=0, tiled=True)  23.8 us
    all_to_all x1, waiting for transfers between devices, filter_band(): lax.all_to_all(flat_rows, 'lon', split_axis=0, concat_axis=1, tiled=True)  19.9 us
  transfers between devices with their start and end apart: 9, of which 3 were waited for; matrix products, arithmetic and copies ran while one was open for 3% of the time, Pallas kernels for 0%

commit v1 on v0

v1 whole, which is shorter than its diff:
```python
import functools
import math

import jax
import jax.numpy as jnp
import numpy as np
from jax import lax
from jax.experimental import pallas as pl
from jax.experimental.pallas import tpu as pltpu
from jax.sharding import PartitionSpec as P

LEV = 8
LANES = 128
SUB = 8
MESH = pl.DeviceIdType.MESH
EXACT = lax.Precision.HIGHEST


def round_up(value, step):
    return -(-value // step) * step


def inner_length(columns):
    return max(a for a in range(1, LANES // LEV + 1) if columns % a == 0)


def dft_tables(length, inner):
    outer = length // inner
    half = outer // 2 + 1
    kept = round_up(half, SUB)
    p = np.arange(outer)
    k1 = np.arange(half)
    angle = 2.0 * np.pi * ((p[None, :] * k1[:, None]) % outer) / outer
    first = np.zeros((2 * kept, outer))
    first[:half] = np.cos(angle)
    first[kept : kept + half] = -np.sin(angle)
    twice = np.where((k1 == 0) | (2 * k1 == outer), 1.0, 2.0)[:, None] / length
    last = np.zeros((outer, 2 * kept))
    last[:, :half] = (twice * np.cos(angle)).T
    last[:, kept : kept + half] = (-twice * np.sin(angle)).T
    a = np.arange(inner)
    turn = 2.0 * np.pi * ((k1[:, None] * a[None, :]) % length) / length
    twiddle = np.zeros((2, kept, LANES))
    twiddle[0, :half, : inner * LEV] = np.repeat(np.cos(turn), LEV, axis=1)
    twiddle[1, :half, : inner * LEV] = np.repeat(-np.sin(turn), LEV, axis=1)
    small = 2.0 * np.pi * ((a[:, None] * a[None, :]) % inner) / inner
    eye = np.eye(LEV)

    def real_form(re, im):
        out = np.zeros((2 * LANES, 2 * LANES))
        used = inner * LEV
        out[:used, :used] = np.kron(re, eye)
        out[:used, LANES : LANES + used] = np.kron(im, eye)
        out[LANES : LANES + used, :used] = -np.kron(im, eye)
        out[LANES : LANES + used, LANES : LANES + used] = np.kron(re, eye)
        return out

    forward = real_form(np.cos(small), -np.sin(small))
    backward = real_form(np.cos(small), np.sin(small))
    k = k1[:, None] + outer * a[None, :]
    wave = np.zeros((kept, LANES))
    wave[:half, : inner * LEV] = np.repeat(np.minimum(k, length - k), LEV, axis=1)
    tables = (first, twiddle, forward, backward, last, wave)
    return [np.asarray(t, np.float32) for t in tables]


def plan(lat_size, lon_size, row_count):
    groups = row_count // SUB
    split = lon_size // groups
    planes = 1 if split == 4 else 2
    slots = 4 // (planes * split)
    return groups, split, planes, slots


def filter_kernel(
    lat_size,
    lon_size,
    inner,
    winds,
    thickness,
    tracer,
    params,
    first,
    twiddle,
    forward,
    backward,
    last,
    wave,
    filt,
    south,
    north,
    recv,
    spread,
    done,
    ret,
    own,
    ext,
    edge,
    edge_in,
    prm,
    fwd_send,
    fwd_recv,
    ret_send,
    ret_recv,
    halo_send,
    halo_recv,
    rim_send,
    own_sem,
    edge_send,
    edge_recv,
    prm_sem,
    filt_sem,
):
    row_count, width = thickness.shape
    padded = filt.shape[-1]
    groups, split, planes, slots = plan(lat_size, lon_size, row_count)
    used = inner * LEV
    pieces = width // used
    outer = pieces * lon_size
    kept = wave.shape[0]
    quarter = lat_size // 4
    bit = 1 << (lat_size.bit_length() - 3)
    polar_bands = [b for b in range(lat_size) if b < quarter or b >= lat_size - quarter]
    band = lax.axis_index("lat")
    lon = lax.axis_index("lon")
    is_polar = (band < quarter) | (band >= lat_size - quarter)
    lowbit = (band // bit) % 2
    partner = band + bit - 2 * bit * lowbit
    home = jnp.where(is_polar, band, partner)
    my_plane = jnp.where(is_polar, 0, 1)
    my_group = lax.rem(lon, groups)
    my_split = lon // groups

    def pair_of(b):
        return {b, b ^ bit} if planes == 2 else {b}

    linked = [[False] * lat_size for _ in range(lat_size)]
    for b in range(lat_size):
        linked[b][b] = True
    for pb in polar_bands:
        for worker in pair_of(pb):
            targets = pair_of(pb) | {t for t in (pb - 1, pb + 1) if 0 <= t < lat_size}
            for target in targets:
                linked[worker][target] = linked[target][worker] = True

    barrier = pltpu.get_barrier_semaphore()
    expected = jnp.int32(-1)
    for other in range(lat_size):
        who = [b for b in range(lat_size) if linked[b][other]]
        talks = functools.reduce(jnp.logical_or, [band == b for b in who])
        expected += jnp.where(talks, lon_size, 0)

        @pl.when(talks)
        def _():
            for step in range(lon_size):
                target = lax.rem(lon + step, lon_size)

                @pl.when((target != lon) | (band != other))
                def _():
                    pl.semaphore_signal(
                        barrier, inc=1, device_id={"lat": other, "lon": target}, device_id_type=MESH
                    )

        near = [b for b in range(lat_size) if abs(b - other) == 1 and not linked[b][other]]
        if near:
            beside = functools.reduce(jnp.logical_or, [band == b for b in near])
            expected += jnp.where(beside, 1, 0)

            @pl.when(beside)
            def _():
                pl.semaphore_signal(
                    barrier, inc=1, device_id={"lat": other, "lon": lon}, device_id_type=MESH
                )

    pl.semaphore_wait(barrier, expected)

    def copies(src, dst, ssem, rsem, lat_to, lon_to):
        remote = pltpu.make_async_remote_copy(
            src_ref=src,
            dst_ref=dst,
            send_sem=ssem,
            recv_sem=rsem,
            device_id={"lat": lat_to, "lon": lon_to},
            device_id_type=MESH,
        )
        local = pltpu.make_async_copy(src, dst, rsem)
        return remote, local

    def push(src, dst, ssem, rsem, lat_to, lon_to):
        remote, local = copies(src, dst, ssem, rsem, lat_to, lon_to)
        same = (lat_to == band) & (lon_to == lon)

        @pl.when(same)
        def _():
            local.start()

        @pl.when(jnp.logical_not(same))
        def _():
            remote.start()

    def sent(src, dst, ssem, rsem, lat_to, lon_to):
        remote, _ = copies(src, dst, ssem, rsem, lat_to, lon_to)
        same = (lat_to == band) & (lon_to == lon)

        @pl.when(jnp.logical_not(same))
        def _():
            remote.wait_send()

    def arrived(dst, rsem):
        pltpu.make_async_copy(dst, dst, rsem).wait()

    fields = [winds.at[0], winds.at[1], thickness, tracer]

    def forward_copies(action):
        for slot in range(slots):
            for step in range(groups):
                group = lax.rem(lon + step, groups)
                for part in range(split):
                    for plane in reversed(range(planes)):
                        target = part * groups + group
                        field = (plane * split + part) * slots + slot
                        rows = pl.ds(pl.multiple_of(group * SUB, SUB), SUB)
                        action(
                            fields[field].at[rows, :],
                            recv.at[slot, lon],
                            fwd_send.at[slot, plane, target],
                            fwd_recv.at[slot, lon],
                            partner if plane else band,
                            target,
                        )

    def param_copy():
        return pltpu.make_async_remote_copy(
            src_ref=params.at[my_group],
            dst_ref=prm,
            send_sem=prm_sem.at[0],
            recv_sem=prm_sem.at[1],
            device_id={"lat": partner, "lon": lon},
            device_id_type=MESH,
        )

    @pl.when(is_polar)
    def _():
        if planes == 2:
            param_copy().start()
        forward_copies(push)

    def edge_copy(side):
        shift = 1 if side else lon_size - 1
        return pltpu.make_async_remote_copy(
            src_ref=edge,
            dst_ref=edge_in.at[side],
            send_sem=edge_send.at[side],
            recv_sem=edge_recv.at[side],
            device_id={"lat": band, "lon": lax.rem(lon + shift, lon_size)},
            device_id_type=MESH,
        )

    def rim_copy(side, item):
        rows = pl.ds(0, SUB) if side == 0 else pl.ds(row_count - SUB, SUB)
        dst = north if side == 0 else south
        return pltpu.make_async_remote_copy(
            src_ref=ext.at[item + 1, rows, :],
            dst_ref=dst.at[item],
            send_sem=rim_send.at[side, item],
            recv_sem=halo_recv.at[1 - side, item],
            device_id={"lat": band - 1 if side == 0 else band + 1, "lon": lon},
            device_id_type=MESH,
        )

    def keep_copy():
        return pltpu.make_async_copy(ext, filt, filt_sem.at[0])

    @pl.when(jnp.logical_not(is_polar))
    def _():
        loads = [pltpu.make_async_copy(fields[f], own.at[f], own_sem.at[f]) for f in range(4)]
        for load in loads:
            load.start()
        for load in loads:
            load.wait()
        for item, f in enumerate((0, 2, 3)):
            edge[item, :, :LEV] = own[f, :, :LEV]
            edge[item, :, LEV : 2 * LEV] = own[f, :, width - LEV :]
        edge_copy(0).start()
        edge_copy(1).start()
        for f in range(4):
            ext[f, :, :width] = own[f]
        edge_copy(0).wait()
        edge_copy(1).wait()
        for item, f in enumerate((0, 2, 3)):
            ext[f, :, width : width + LEV] = edge_in[0, item, :, :LEV]
            ext[f, :, padded - LEV :] = edge_in[1, item, :, LEV : 2 * LEV]
        keep_copy().start()
        for side in range(2):
            for item in range(3):
                rim_copy(side, item).start()

    def return_copies(slot, action):
        field = (my_plane * split + my_split) * slots + slot
        rows = pl.ds(pl.multiple_of(my_group * SUB, SUB), SUB)
        for step in range(lon_size):
            target = lax.rem(lon + step, lon_size)
            action(
                ret.at[slot, target],
                filt.at[field, rows, :],
                ret_send.at[slot, target],
                ret_recv.at[slot, my_plane, lon],
                home,
                target,
            )
        item = jnp.maximum(field - 1, 0)
        opposite = lon_size // 2
        for side in range(2):
            at_edge = my_group == (0 if side == 0 else groups - 1)
            at_pole = home == (0 if side == 0 else lat_size - 1)
            lat_to = home - 1 if side == 0 else home + 1

            @pl.when(at_edge & (field >= 1) & jnp.logical_not(at_pole))
            def _():
                for target in range(lon_size):
                    action(
                        ret.at[slot, target],
                        (north if side == 0 else south).at[item],
                        halo_send.at[slot, side, target],
                        halo_recv.at[1 - side, item],
                        lat_to,
                        jnp.int32(target),
                    )

            @pl.when(at_edge & (field == 2) & at_pole)
            def _():
                for target in range(lon_size):
                    action(
                        ret.at[slot, target],
                        (south if side == 0 else north).at[1],
                        halo_send.at[slot, side, target],
                        halo_recv.at[side, 1],
                        home,
                        jnp.int32((target + opposite) % lon_size),
                    )

    batch = 4

    def work(slot):
        for s in range(lon_size):
            arrived(recv.at[slot, s], fwd_recv.at[slot, s])

        def spread_sector(s, carry):
            block = recv[slot, s]
            for p in range(pieces):
                piece = block[:, used * p : used * (p + 1)]
                if used < LANES:
                    blank = jnp.zeros((SUB, LANES - used), jnp.float32)
                    piece = jnp.concatenate([piece, blank], axis=1)
                spread[pl.ds(s * pieces + p, SUB, stride=outer), :] = piece
            return carry

        lax.fori_loop(0, lon_size, spread_sector, 0)

        def some_rows(step, carry):
            base = step * batch
            rows = [spread[pl.ds((base + j) * outer, outer), :] for j in range(batch)]
            x = jnp.concatenate(rows, axis=1)
            y = jnp.dot(first[...], x, precision=EXACT, preferred_element_type=jnp.float32)
            tr, ti = twiddle[0], twiddle[1]
            z = []
            for j in range(batch):
                yr = y[:kept, j * LANES : (j + 1) * LANES]
                yi = y[kept:, j * LANES : (j + 1) * LANES]
                z.append(jnp.concatenate([yr * tr - yi * ti, yr * ti + yi * tr], axis=1))
            z = jnp.concatenate(z, axis=0)
            spectrum = jnp.dot(z, forward[...], precision=EXACT, preferred_element_type=jnp.float32)
            k = wave[...]
            inverse_k = 1.0 / jnp.maximum(k, 1.0)
            weighted = []
            for j in range(batch):
                cut = prm[pl.ds(base + j, 1), :]
                damp = prm[pl.ds(SUB + base + j, 1), :]
                ratio = cut * inverse_k
                factor = jnp.where(k > cut, damp * ratio * ratio, 1.0)
                weighted.append(
                    spectrum[j * kept : (j + 1) * kept] * jnp.concatenate([factor, factor], axis=1)
                )
            weighted = jnp.concatenate(weighted, axis=0)
            v = jnp.dot(weighted, backward[...], precision=EXACT, preferred_element_type=jnp.float32)
            u = []
            for j in range(batch):
                vr = v[j * kept : (j + 1) * kept, :LANES]
                vi = v[j * kept : (j + 1) * kept, LANES:]
                u.append(jnp.concatenate([vr * tr + vi * ti, vi * tr - vr * ti], axis=0))
            u = jnp.concatenate(u, axis=1)
            out = jnp.dot(last[...], u, precision=EXACT, preferred_element_type=jnp.float32)
            for j in range(batch):
                done[pl.ds((base + j) * outer, outer), :] = out[:, j * LANES : (j + 1) * LANES]
            return carry

        lax.fori_loop(0, SUB // batch, some_rows, 0)

        def gather_sector(s, carry):
            for p in range(pieces):
                piece = done[pl.ds(s * pieces + p, SUB, stride=outer), :]
                ret[slot, s, :, used * p : used * (p + 1)] = piece[:, :used]
            east = lax.rem(s + 1, lon_size) * pieces
            west = lax.rem(s + lon_size - 1, lon_size) * pieces + pieces - 1
            ret[slot, s, :, width : width + LEV] = done[pl.ds(east, SUB, stride=outer), :][:, :LEV]
            ret[slot, s, :, padded - LEV :] = done[pl.ds(west, SUB, stride=outer), :][
                :, used - LEV : used
            ]
            return carry

        lax.fori_loop(0, lon_size, gather_sector, 0)
        return_copies(slot, push)

    def all_work():
        for slot in range(slots):
            work(slot)
        for slot in range(slots):
            return_copies(slot, sent)

    @pl.when(is_polar)
    def _():
        prm[...] = params[my_group]

    if planes == 2:

        @pl.when(jnp.logical_not(is_polar))
        def _():
            param_copy().wait_recv()

        all_work()
    else:
        pl.when(is_polar)(all_work)

    @pl.when(is_polar)
    def _():
        if planes == 2:
            param_copy().wait_send()
        forward_copies(sent)
        for slot in range(slots):
            for plane in range(planes):
                for source in range(lon_size):
                    field = (plane * split + source // groups) * slots + slot
                    row = (source % groups) * SUB
                    arrived(
                        filt.at[field, pl.ds(row, SUB), :], ret_recv.at[slot, plane, source]
                    )

    @pl.when(jnp.logical_not(is_polar))
    def _():
        keep_copy().wait()
        for side in range(2):
            for item in range(3):
                rim_copy(side, item).wait_send()

    for side, rim in enumerate((south, north)):
        at_pole = band == (0 if side == 0 else lat_size - 1)
        arrived(rim.at[1], halo_recv.at[side, 1])

        @pl.when(jnp.logical_not(at_pole))
        def _():
            arrived(rim.at[0], halo_recv.at[side, 0])
            arrived(rim.at[2], halo_recv.at[side, 2])


def stencil_kernel(
    steps, lat_size, ratio, where_ref, here, below, above, south, north, coef, uv, new_h, new_q
):
    step = pl.program_id(0)
    band = where_ref[0]
    width = new_h.shape[-1]
    padded = here.shape[-1]
    first, final = step == 0, step == steps - 1
    low_pole = first & (band == 0)
    high_pole = final & (band == lat_size - 1)
    u, v, h, q = here[0], here[1], here[2], here[3]

    def south_of(x, item):
        row = jnp.where(first, south[item, SUB - 1 : SUB, :], below[item + 1, SUB - 1 : SUB, :])
        pole = south[1, 0:1, :] if item == 1 else jnp.zeros_like(row)
        row = jnp.where(low_pole, pole, row)
        return jnp.concatenate([row, x[: SUB - 1]], axis=0)

    def north_of(x, item):
        row = jnp.where(final, north[item, 0:1, :], above[item + 1, 0:1, :])
        pole = north[1, SUB - 1 : SUB, :] if item == 1 else jnp.zeros_like(row)
        row = jnp.where(high_pole, pole, row)
        return jnp.concatenate([x[1:], row], axis=0)

    def east_of(x):
        return pltpu.roll(x, padded - LEV, 1)

    def west_of(x):
        return pltpu.roll(x, LEV, 1)

    inv_c = coef[:, 0:1]
    face_s = coef[:, 1:2]
    face_n = coef[:, 2:3]
    he, hs, hn = east_of(h), south_of(h, 1), north_of(h, 1)
    hw = west_of(h)
    wind = 0.25 * (u + east_of(u))
    fx = wind * (h + he)
    gx = wind * (q + east_of(q))
    wind_s = face_s * (south_of(v, 0) + v)
    wind_n = face_n * (v + north_of(v, 0))
    fy = wind_n * (h + hn) - wind_s * (hs + h)
    gy = wind_n * (q + north_of(q, 2)) - wind_s * (south_of(q, 2) + q)
    out_h = h - ((fx - west_of(fx)) + fy) * inv_c
    out_q = q - ((gx - west_of(gx)) + gy) * inv_c
    out_u = u - (he - hw) * (0.5 * inv_c)
    out_v = v - (hn - hs) * (0.5 * ratio)
    uv[0] = out_u[:, :width]
    uv[1] = out_v[:, :width]
    new_h[...] = out_h[:, :width]
    new_q[...] = out_q[:, :width]


def per_device(winds, thickness, tracer, cutoff, damping):
    lat_size = lax.axis_size("lat")
    lon_size = lax.axis_size("lon")
    band = lax.axis_index("lat")
    row_count, width = thickness.shape
    columns = width // LEV
    length = columns * lon_size
    nlat = row_count * lat_size
    inner = inner_length(columns)
    outer = length // inner
    padded = round_up(width + 2 * LEV, LANES)
    groups, split, planes, slots = plan(lat_size, lon_size, row_count)
    params = jnp.stack([cutoff.astype(jnp.float32), damping]).reshape(2, groups, SUB)
    params = jnp.transpose(params, (1, 0, 2)).reshape(groups, 2 * SUB, 1)
    params = jnp.broadcast_to(params, (groups, 2 * SUB, LANES))
    tables = [jnp.asarray(t) for t in dft_tables(length, inner)]
    any_spec = pl.BlockSpec(memory_space=pl.ANY)
    vmem_spec = pl.BlockSpec(memory_space=pltpu.VMEM)
    f32 = jnp.float32
    filt, south, north = pl.pallas_call(
        functools.partial(filter_kernel, lat_size, lon_size, inner),
        out_shape=(
            jax.ShapeDtypeStruct((4, row_count, padded), f32),
            jax.ShapeDtypeStruct((3, SUB, padded), f32),
            jax.ShapeDtypeStruct((3, SUB, padded), f32),
        ),
        in_specs=[any_spec] * 3 + [vmem_spec] * (1 + len(tables)),
        out_specs=(any_spec,) * 3,
        scratch_shapes=[
            pltpu.VMEM((slots, lon_size, SUB, width), f32),
            pltpu.VMEM((SUB * outer, LANES), f32),
            pltpu.VMEM((SUB * outer, LANES), f32),
            pltpu.VMEM((slots, lon_size, SUB, padded), f32),
            pltpu.VMEM((4, row_count, width), f32),
            pltpu.VMEM((4, row_count, padded), f32),
            pltpu.VMEM((3, row_count, LANES), f32),
            pltpu.VMEM((2, 3, row_count, LANES), f32),
            pltpu.VMEM((2 * SUB, LANES), f32),
            pltpu.SemaphoreType.DMA((slots, planes, lon_size)),
            pltpu.SemaphoreType.DMA((slots, lon_size)),
            pltpu.SemaphoreType.DMA((slots, lon_size)),
            pltpu.SemaphoreType.DMA((slots, 2, lon_size)),
            pltpu.SemaphoreType.DMA((slots, 2, lon_size)),
            pltpu.SemaphoreType.DMA((2, 3)),
            pltpu.SemaphoreType.DMA((2, 3)),
            pltpu.SemaphoreType.DMA((4,)),
            pltpu.SemaphoreType.DMA((2,)),
            pltpu.SemaphoreType.DMA((2,)),
            pltpu.SemaphoreType.DMA((2,)),
            pltpu.SemaphoreType.DMA((1,)),
        ],
        compiler_params=pltpu.CompilerParams(
            collective_id=0, has_side_effects=True, vmem_limit_bytes=48 * 1024 * 1024
        ),
        cost_estimate=pl.CostEstimate(
            flops=4 * 10**9, bytes_accessed=4 * row_count * padded * 8, transcendentals=0
        ),
        name="polar_filter",
    )(winds, thickness, tracer, params, *tables)

    dlam = 2.0 * math.pi / length
    dphi = math.pi / nlat
    ratio = dlam / dphi
    rows = band * row_count + jnp.arange(row_count, dtype=jnp.int32)
    cos_center = jnp.cos(-math.pi / 2 + (rows.astype(f32) + 0.5) * dphi)

    def face(m):
        cosine = jnp.cos(-math.pi / 2 + m.astype(f32) * dphi)
        return jnp.where((m == 0) | (m == nlat), 0.0, cosine)

    coef = jnp.stack(
        [1.0 / cos_center, 0.25 * ratio * face(rows), 0.25 * ratio * face(rows + 1)], axis=1
    )
    steps = row_count // SUB
    where_am_i = band.astype(jnp.int32).reshape(1)
    block = (4, SUB, padded)
    whole = (3, SUB, padded)
    uv, new_h, new_q = pl.pallas_call(
        functools.partial(stencil_kernel, steps, lat_size, ratio),
        grid=(steps,),
        out_shape=(
            jax.ShapeDtypeStruct((2, row_count, width), f32),
            jax.ShapeDtypeStruct((row_count, width), f32),
            jax.ShapeDtypeStruct((row_count, width), f32),
        ),
        in_specs=[
            pl.BlockSpec(memory_space=pltpu.SMEM),
            pl.BlockSpec(block, lambda i: (0, i, 0)),
            pl.BlockSpec(block, lambda i: (0, jnp.maximum(i - 1, 0), 0)),
            pl.BlockSpec(block, lambda i: (0, jnp.minimum(i + 1, steps - 1), 0)),
            pl.BlockSpec(whole, lambda i: (0, 0, 0)),
            pl.BlockSpec(whole, lambda i: (0, 0, 0)),
            pl.BlockSpec((SUB, 3), lambda i: (i, 0)),
        ],
        out_specs=(
            pl.BlockSpec((2, SUB, width), lambda i: (0, i, 0)),
            pl.BlockSpec((SUB, width), lambda i: (i, 0)),
            pl.BlockSpec((SUB, width), lambda i: (i, 0)),
        ),
        compiler_params=pltpu.CompilerParams(vmem_limit_bytes=32 * 1024 * 1024),
        name="stencil",
    )(where_am_i, filt, filt, filt, south, north, coef)
    return uv, new_h, new_q


def solution(mesh):
    placed = (P(None, "lat", "lon"), P("lat", "lon"), P("lat", "lon"), P("lat"), P("lat"))
    return jax.shard_map(
        per_device,
        mesh=mesh,
        in_specs=placed,
        out_specs=(P(None, "lat", "lon"), P("lat", "lon"), P("lat", "lon")),
        check_vma=False,
    )
```

time: 527 us -> 93 us (0.18)
  the two profiles are of different devices: /device:TPU:0 before, /device:TPU:7 now
where the time goes in v1:
time: 93 us; the launch traced here: 92.5 us
  Pallas kernels  79 us (85%)
  local copies, waits for them, and re-layouts  12 us (13%)
    pallas_call x1, Pallas kernels, per_device(): pl.pallas_call(functools.partial(filter_kernel, lat_size, lon_size, inner...  74.1 us
    unnamed x20, local copies, waits for them, and re-layouts  10.9 us
    pallas_call x1, Pallas kernels, per_device(): pl.pallas_call(functools.partial(stencil_kernel, steps, lat_size, ratio),...  4.88 us

profile of v1, /device:TPU:7, one launch (start us, length us, event | category | flops | bytes accessed | tf_op | source)
XLA Modules:
  0.0 92.5 jit_solution(5983656471507843467)
XLA Ops:
  0.6 0.7 convert_element_type.28
  1.3 0.1 fusion
  1.4 0.1 stack.15
  1.5 0.7 stack.16
  2.3 0.1 broadcast_in_dim.12
  2.3 0.1 copy.16.coef
  2.4 0.1 broadcast_in_dim.13.params
  2.5 0.0 copy-start.1
  2.5 1.4 %copy-done.1 = f32[2,64,2880]{2,1,0:T(8,128)S(1)} copy-done((f32[2,64,2880]{2,1,0:T(8,128)S(1)}, f32[2,64,2880]{2,1,0:T(8,128)}, u32[]{:S(2)}) %copy-start.1) | copy-done | bytes 1474584
  3.9 0.0 copy-start.2
  3.9 1.1 %copy-done.2 = f32[64,2880]{1,0:T(8,128)S(1)} copy-done((f32[64,2880]{1,0:T(8,128)S(1)}, f32[64,2880]{1,0:T(8,128)}, u32[]{:S(2)}) %copy-start.2) | copy-done | bytes 737304
  5.0 0.0 copy-start.3
  5.0 1.1 %copy-done.3 = f32[64,2880]{1,0:T(8,128)S(1)} copy-done((f32[64,2880]{1,0:T(8,128)S(1)}, f32[64,2880]{1,0:T(8,128)}, u32[]{:S(2)}) %copy-start.3) | copy-done | bytes 737304
  6.1 0.0 copy-start.4
  6.2 0.9 %copy-done.4 = f32[256,256]{1,0:T(8,128)S(1)} copy-done((f32[256,256]{1,0:T(8,128)S(1)}, f32[256,256]{1,0:T(8,128)}, u32[]{:S(2)}) %copy-start.4) | copy-done | bytes 262168
  7.1 0.9 %copy-done.5 = f32[256,256]{1,0:T(8,128)S(1)} copy-done((f32[256,256]{1,0:T(8,128)S(1)}, f32[256,256]{1,0:T(8,128)}, u32[]{:S(2)}) %copy-start.5) | copy-done | bytes 262168
  8.1 0.9 %copy-done.6 = f32[208,192]{1,0:T(8,128)S(1)} copy-done((f32[208,192]{1,0:T(8,128)S(1)}, f32[208,192]{1,0:T(8,128)}, u32[]{:S(2)}) %copy-start.6) | copy-done | bytes 159768
  9.0 0.9 copy-done.7
  9.9 0.9 copy-done.8
  10.8 0.8 copy-done.9
  11.6 74.1 %polar_filter.1 = (f32[4,64,2944]{2,1,0:T(8,128)}, f32[3,8,2944]{2,1,0:T(8,128)S(1)}, f32[3,8,2944]{2,1,0:T(8,128)S(1)}) custom-call(f32[2,64,2880]{2,1,0:T(8,128)S(1)} %copy-done.1, f32[64,2880]{1,0:T(8,128)S(1)} %copy-done.2, f32[64,2880]{1,0:T(8,128)S(1)} %copy-done.3, f32[8,16,128]{2,1,0:T(8,128)S(1)} %broadcast_in_dim.13.params, ...), custom_call_target="tpu_custom_call" | custom-call | flops 4000000000 | bytes 6029312 | tf_op jit(solution)/shard_map/polar_filter/pallas_call | solution.py:536
  85.7 0.0 copy-start
  85.8 1.8 %copy-done = f32[4,64,2944]{2,1,0:T(8,128)S(1)} copy-done((f32[4,64,2944]{2,1,0:T(8,128)S(1)}, f32[4,64,2944]{2,1,0:T(8,128)}, u32[]{:S(2)}) %copy-start) | copy-done | bytes 3014680
  87.6 4.9 %stencil.1 = (f32[2,64,2880]{2,1,0:T(8,128)}, f32[64,2880]{1,0:T(8,128)}, f32[64,2880]{1,0:T(8,128)}) custom-call(s32[1]{0:T(128)} %bitcast.where_ref, f32[4,64,2944]{2,1,0:T(8,128)S(1)} %copy-done, f32[4,64,2944]{2,1,0:T(8,128)S(1)} %copy-done, f32[4,64,2944]{2,1,0:T(8,128)S(1)} %copy-done, f32[3,8,2944]{2,1,0:T(8,128)S(1)} %get-tuple-element.7.south, ...), custom_call_target="tpu_custom_call" | custom-call | tf_op jit(solution)/shard_map/stencil/pallas_call | solution.py:594
  (9 shorter events, 0.1 us)
Async XLA Ops:
  2.5 1.4 %copy-start.1 = (f32[2,64,2880]{2,1,0:T(8,128)S(1)}, f32[2,64,2880]{2,1,0:T(8,128)}, u32[]{:S(2)}) copy-start(f32[2,64,2880]{2,1,0:T(8,128)} %winds.1) | copy-start | bytes 4423684
  3.9 1.1 %copy-start.2 = (f32[64,2880]{1,0:T(8,128)S(1)}, f32[64,2880]{1,0:T(8,128)}, u32[]{:S(2)}) copy-start(f32[64,2880]{1,0:T(8,128)} %thickness.1) | copy-start | bytes 2211844
  5.0 1.1 %copy-start.3 = (f32[64,2880]{1,0:T(8,128)S(1)}, f32[64,2880]{1,0:T(8,128)}, u32[]{:S(2)}) copy-start(f32[64,2880]{1,0:T(8,128)} %tracer.1) | copy-start | bytes 2211844
  6.1 0.9 %copy-start.4 = (f32[256,256]{1,0:T(8,128)S(1)}, f32[256,256]{1,0:T(8,128)}, u32[]{:S(2)}) copy-start(f32[256,256]{1,0:T(8,128)} %constant.40.clone.backward) | copy-start | bytes 786436
  7.1 0.9 %copy-start.5 = (f32[256,256]{1,0:T(8,128)S(1)}, f32[256,256]{1,0:T(8,128)}, u32[]{:S(2)}) copy-start(f32[256,256]{1,0:T(8,128)} %constant.39.clone.forward) | copy-start | bytes 786436
  8.0 0.9 %copy-start.6 = (f32[208,192]{1,0:T(8,128)S(1)}, f32[208,192]{1,0:T(8,128)}, u32[]{:S(2)}) copy-start(f32[208,192]{1,0:T(8,128)} %constant.37.clone.first) | copy-start | bytes 479236
  9.0 0.9 %copy-start.7 = (f32[192,208]{1,0:T(8,128)S(1)}, f32[192,208]{1,0:T(8,128)}, u32[]{:S(2)}) copy-start(f32[192,208]{1,0:T(8,128)} %constant.41.clone.last) | copy-start | bytes 479236
  9.9 0.9 copy-start.8
  10.8 0.8 copy-start.9
  85.7 1.9 %copy-start = (f32[4,64,2944]{2,1,0:T(8,128)S(1)}, f32[4,64,2944]{2,1,0:T(8,128)}, u32[]{:S(2)}) copy-start(f32[4,64,2944]{2,1,0:T(8,128)} %get-tuple-element.6.here.below.above) | copy-start | bytes 9043972

commit v2 on v1

--- a/solution.py
+++ b/solution.py
@@ -13,6 +13,7 @@
 LANES = 128
 SUB = 8
 MESH = pl.DeviceIdType.MESH
+TABLES = 7
 EXACT = lax.Precision.HIGHEST
 
 
@@ -22,6 +23,23 @@
 
 def inner_length(columns):
     return max(a for a in range(1, LANES // LEV + 1) if columns % a == 0)
+
+
+def halves(x):
+    high = x.astype(jnp.bfloat16)
+    return high, (x - high.astype(jnp.float32)).astype(jnp.bfloat16)
+
+
+def left_dot(parts, x):
+    high, low = halves(x)
+    stacked = jnp.concatenate([high, low, high], axis=0)
+    return jnp.dot(parts[...], stacked, preferred_element_type=jnp.float32)
+
+
+def right_dot(x, parts):
+    high, low = halves(x)
+    stacked = jnp.concatenate([high, low, high], axis=1)
+    return jnp.dot(stacked, parts[...], preferred_element_type=jnp.float32)
 
 
 def dft_tables(length, inner):
@@ -60,8 +78,19 @@
     k = k1[:, None] + outer * a[None, :]
     wave = np.zeros((kept, LANES))
     wave[:half, : inner * LEV] = np.repeat(np.minimum(k, length - k), LEV, axis=1)
-    tables = (first, twiddle, forward, backward, last, wave)
-    return [np.asarray(t, np.float32) for t in tables]
+    average = np.zeros((LANES, LANES))
+    average[: inner * LEV, : inner * LEV] = np.kron(np.ones((inner, inner)), eye) / length
+
+    def left_parts(table):
+        high, low = halves(np.asarray(table, np.float32))
+        return np.concatenate([high, high, low], axis=1)
+
+    def right_parts(table):
+        high, low = halves(np.asarray(table, np.float32))
+        return np.concatenate([high, high, low], axis=0)
+
+    matrices = [left_parts(first), right_parts(forward), right_parts(backward), left_parts(last)]
+    return matrices + [np.asarray(t, np.float32) for t in (twiddle, wave, average)]
 
 
 def plan(lat_size, lon_size, row_count):
@@ -79,17 +108,17 @@
     winds,
     thickness,
     tracer,
-    params,
-    first,
-    twiddle,
-    forward,
-    backward,
-    last,
-    wave,
-    filt,
-    south,
-    north,
-    recv,
+    cutoff,
+    damping,
+    *rest,
+):
+    table_in, rest = rest[:TABLES], rest[TABLES:]
+    (filt, south, north), rest = rest[:3], rest[3:]
+    tables, rest = rest[:TABLES], rest[TABLES:]
+    first, forward, backward, last, twiddle, wave, average = tables
+    (
+
+        recv,
     spread,
     done,
     ret,
@@ -110,7 +139,8 @@
     edge_recv,
     prm_sem,
     filt_sem,
-):
+    table_sem,
+    ) = rest
     row_count, width = thickness.shape
     padded = filt.shape[-1]
     groups, split, planes, slots = plan(lat_size, lon_size, row_count)
@@ -143,6 +173,13 @@
             for target in targets:
                 linked[worker][target] = linked[target][worker] = True
 
+    table_loads = [
+        pltpu.make_async_copy(table_in[i], tables[i], table_sem.at[i]) for i in range(TABLES)
+    ]
+    arrays = [winds.at[0], winds.at[1], thickness, tracer]
+    loads = [pltpu.make_async_copy(arrays[f], own.at[f], own_sem.at[f]) for f in range(4)]
+    for load in loads + table_loads:
+        load.start()
     barrier = pltpu.get_barrier_semaphore()
     expected = jnp.int32(-1)
     for other in range(lat_size):
@@ -209,29 +246,29 @@
     def arrived(dst, rsem):
         pltpu.make_async_copy(dst, dst, rsem).wait()
 
-    fields = [winds.at[0], winds.at[1], thickness, tracer]
-
-    def forward_copies(action):
-        for slot in range(slots):
-            for step in range(groups):
-                group = lax.rem(lon + step, groups)
-                for part in range(split):
-                    for plane in reversed(range(planes)):
-                        target = part * groups + group
-                        field = (plane * split + part) * slots + slot
-                        rows = pl.ds(pl.multiple_of(group * SUB, SUB), SUB)
-                        action(
-                            fields[field].at[rows, :],
-                            recv.at[slot, lon],
-                            fwd_send.at[slot, plane, target],
-                            fwd_recv.at[slot, lon],
-                            partner if plane else band,
-                            target,
-                        )
+    def forward_copies(slot, action):
+        for step in range(groups):
+            group = lax.rem(lon + step, groups)
+            for part in range(split):
+                for plane in reversed(range(planes)):
+                    target = part * groups + group
+                    field = (plane * split + part) * slots + slot
+                    rows = pl.ds(pl.multiple_of(group * SUB, SUB), SUB)
+                    action(
+                        own.at[field, rows, :],
+                        recv.at[slot, lon],
+                        fwd_send.at[slot, plane, target],
+                        fwd_recv.at[slot, lon],
+                        partner if plane else band,
+                        target,
+                    )
+
+    for load in loads:
+        load.wait()
 
     def param_copy():
         return pltpu.make_async_remote_copy(
-            src_ref=params.at[my_group],
+            src_ref=prm,
             dst_ref=prm,
             send_sem=prm_sem.at[0],
             recv_sem=prm_sem.at[1],
@@ -241,9 +278,13 @@
 
     @pl.when(is_polar)
     def _():
+        forward_copies(0, push)
+        for j in range(SUB):
+            row = my_group * SUB + j
+            prm[j : j + 1, :] = jnp.full((1, LANES), cutoff[row].astype(jnp.float32))
+            prm[SUB + j : SUB + j + 1, :] = jnp.full((1, LANES), damping[row])
         if planes == 2:
             param_copy().start()
-        forward_copies(push)
 
     def edge_copy(side):
         shift = 1 if side else lon_size - 1
@@ -273,11 +314,6 @@
 
     @pl.when(jnp.logical_not(is_polar))
     def _():
-        loads = [pltpu.make_async_copy(fields[f], own.at[f], own_sem.at[f]) for f in range(4)]
-        for load in loads:
-            load.start()
-        for load in loads:
-            load.wait()
         for item, f in enumerate((0, 2, 3)):
             edge[item, :, :LEV] = own[f, :, :LEV]
             edge[item, :, LEV : 2 * LEV] = own[f, :, width - LEV :]
@@ -360,8 +396,16 @@
         def some_rows(step, carry):
             base = step * batch
             rows = [spread[pl.ds((base + j) * outer, outer), :] for j in range(batch)]
-            x = jnp.concatenate(rows, axis=1)
-            y = jnp.dot(first[...], x, precision=EXACT, preferred_element_type=jnp.float32)
+            sums = [jnp.sum(row, axis=0, keepdims=True) for row in rows] * (SUB // batch)
+            mean = jnp.dot(
+                jnp.concatenate(sums, axis=0),
+                average[...],
+                precision=EXACT,
+                preferred_element_type=jnp.float32,
+            )
+            means = [mean[j : j + 1] for j in range(batch)]
+            x = jnp.concatenate([rows[j] - means[j] for j in range(batch)], axis=1)
+            y = left_dot(first, x)
             tr, ti = twiddle[0], twiddle[1]
             z = []
             for j in range(batch):
@@ -369,7 +413,7 @@
                 yi = y[kept:, j * LANES : (j + 1) * LANES]
                 z.append(jnp.concatenate([yr * tr - yi * ti, yr * ti + yi * tr], axis=1))
             z = jnp.concatenate(z, axis=0)
-            spectrum = jnp.dot(z, forward[...], precision=EXACT, preferred_element_type=jnp.float32)
+            spectrum = right_dot(z, forward)
             k = wave[...]
             inverse_k = 1.0 / jnp.maximum(k, 1.0)
             weighted = []
@@ -382,16 +426,17 @@
                     spectrum[j * kept : (j + 1) * kept] * jnp.concatenate([factor, factor], axis=1)
                 )
             weighted = jnp.concatenate(weighted, axis=0)
-            v = jnp.dot(weighted, backward[...], precision=EXACT, preferred_element_type=jnp.float32)
+            v = right_dot(weighted, backward)
             u = []
             for j in range(batch):
                 vr = v[j * kept : (j + 1) * kept, :LANES]
                 vi = v[j * kept : (j + 1) * kept, LANES:]
                 u.append(jnp.concatenate([vr * tr + vi * ti, vi * tr - vr * ti], axis=0))
             u = jnp.concatenate(u, axis=1)
-            out = jnp.dot(last[...], u, precision=EXACT, preferred_element_type=jnp.float32)
+            out = left_dot(last, u)
             for j in range(batch):
-                done[pl.ds((base + j) * outer, outer), :] = out[:, j * LANES : (j + 1) * LANES]
+                piece = out[:, j * LANES : (j + 1) * LANES] + means[j]
+                done[pl.ds((base + j) * outer, outer), :] = piece
             return carry
 
         lax.fori_loop(0, SUB // batch, some_rows, 0)
@@ -413,13 +458,19 @@
 
     def all_work():
         for slot in range(slots):
+            if slot + 1 < slots:
+
+                @pl.when(is_polar)
+                def _():
+                    forward_copies(slot, sent)
+                    forward_copies(slot + 1, push)
+
             work(slot)
         for slot in range(slots):
             return_copies(slot, sent)
 
-    @pl.when(is_polar)
-    def _():
-        prm[...] = params[my_group]
+    for load in table_loads:
+        load.wait()
 
     if planes == 2:
 
@@ -435,7 +486,7 @@
     def _():
         if planes == 2:
             param_copy().wait_send()
-        forward_copies(sent)
+        forward_copies(slots - 1, sent)
         for slot in range(slots):
             for plane in range(planes):
                 for source in range(lon_size):
@@ -526,12 +577,10 @@
     outer = length // inner
     padded = round_up(width + 2 * LEV, LANES)
     groups, split, planes, slots = plan(lat_size, lon_size, row_count)
-    params = jnp.stack([cutoff.astype(jnp.float32), damping]).reshape(2, groups, SUB)
-    params = jnp.transpose(params, (1, 0, 2)).reshape(groups, 2 * SUB, 1)
-    params = jnp.broadcast_to(params, (groups, 2 * SUB, LANES))
     tables = [jnp.asarray(t) for t in dft_tables(length, inner)]
-    any_spec = pl.BlockSpec(memory_space=pl.ANY)
     vmem_spec = pl.BlockSpec(memory_space=pltpu.VMEM)
+    hbm_spec = pl.BlockSpec(memory_space=pltpu.HBM)
+    smem_spec = pl.BlockSpec(memory_space=pltpu.SMEM)
     f32 = jnp.float32
     filt, south, north = pl.pallas_call(
         functools.partial(filter_kernel, lat_size, lon_size, inner),
@@ -540,9 +589,10 @@
             jax.ShapeDtypeStruct((3, SUB, padded), f32),
             jax.ShapeDtypeStruct((3, SUB, padded), f32),
         ),
-        in_specs=[any_spec] * 3 + [vmem_spec] * (1 + len(tables)),
-        out_specs=(any_spec,) * 3,
-        scratch_shapes=[
+        in_specs=[hbm_spec] * 3 + [smem_spec] * 2 + [hbm_spec] * TABLES,
+        out_specs=(vmem_spec,) * 3,
+        scratch_shapes=[pltpu.VMEM(t.shape, t.dtype) for t in tables]
+        + [
             pltpu.VMEM((slots, lon_size, SUB, width), f32),
             pltpu.VMEM((SUB * outer, LANES), f32),
             pltpu.VMEM((SUB * outer, LANES), f32),
@@ -564,56 +614,54 @@
             pltpu.SemaphoreType.DMA((2,)),
             pltpu.SemaphoreType.DMA((2,)),
             pltpu.SemaphoreType.DMA((1,)),
+            pltpu.SemaphoreType.DMA((TABLES,)),
         ],
         compiler_params=pltpu.CompilerParams(
-            collective_id=0, has_side_effects=True, vmem_limit_bytes=48 * 1024 * 1024
+            collective_id=0, has_side_effects=True, vmem_limit_bytes=54 * 1024 * 1024
         ),
         cost_estimate=pl.CostEstimate(
             flops=4 * 10**9, bytes_accessed=4 * row_count * padded * 8, transcendentals=0
         ),
         name="polar_filter",
-    )(winds, thickness, tracer, params, *tables)
+    )(winds, thickness, tracer, cutoff, damping, *tables)
 
     dlam = 2.0 * math.pi / length
     dphi = math.pi / nlat
     ratio = dlam / dphi
-    rows = band * row_count + jnp.arange(row_count, dtype=jnp.int32)
-    cos_center = jnp.cos(-math.pi / 2 + (rows.astype(f32) + 0.5) * dphi)
-
-    def face(m):
-        cosine = jnp.cos(-math.pi / 2 + m.astype(f32) * dphi)
-        return jnp.where((m == 0) | (m == nlat), 0.0, cosine)
-
-    coef = jnp.stack(
-        [1.0 / cos_center, 0.25 * ratio * face(rows), 0.25 * ratio * face(rows + 1)], axis=1
-    )
+    centers = np.cos(-np.pi / 2 + (np.arange(nlat) + 0.5) * dphi)
+    faces = np.cos(-np.pi / 2 + np.arange(nlat + 1) * dphi)
+    faces[0] = faces[-1] = 0.0
+    faces = 0.25 * ratio * faces
+    coef = jnp.asarray(np.stack([1.0 / centers, faces[:-1], faces[1:]], axis=1), f32)
     steps = row_count // SUB
     where_am_i = band.astype(jnp.int32).reshape(1)
     block = (4, SUB, padded)
     whole = (3, SUB, padded)
     uv, new_h, new_q = pl.pallas_call(
         functools.partial(stencil_kernel, steps, lat_size, ratio),
-        grid=(steps,),
+        grid_spec=pltpu.PrefetchScalarGridSpec(
+            num_scalar_prefetch=1,
+            grid=(steps,),
+            in_specs=[
+                pl.BlockSpec(block, lambda i, b: (0, i, 0)),
+                pl.BlockSpec(block, lambda i, b: (0, jnp.maximum(i - 1, 0), 0)),
+                pl.BlockSpec(block, lambda i, b: (0, jnp.minimum(i + 1, steps - 1), 0)),
+                pl.BlockSpec(whole, lambda i, b: (0, 0, 0)),
+                pl.BlockSpec(whole, lambda i, b: (0, 0, 0)),
+                pl.BlockSpec((SUB, 3), lambda i, b: (b[0] * steps + i, 0)),
+            ],
+            out_specs=(
+                pl.BlockSpec((2, SUB, width), lambda i, b: (0, i, 0)),
+                pl.BlockSpec((SUB, width), lambda i, b: (i, 0)),
+                pl.BlockSpec((SUB, width), lambda i, b: (i, 0)),
+            ),
+        ),
         out_shape=(
             jax.ShapeDtypeStruct((2, row_count, width), f32),
             jax.ShapeDtypeStruct((row_count, width), f32),
             jax.ShapeDtypeStruct((row_count, width), f32),
         ),
-        in_specs=[
-            pl.BlockSpec(memory_space=pltpu.SMEM),
-            pl.BlockSpec(block, lambda i: (0, i, 0)),
-            pl.BlockSpec(block, lambda i: (0, jnp.maximum(i - 1, 0), 0)),
-            pl.BlockSpec(block, lambda i: (0, jnp.minimum(i + 1, steps - 1), 0)),
-            pl.BlockSpec(whole, lambda i: (0, 0, 0)),
-            pl.BlockSpec(whole, lambda i: (0, 0, 0)),
-            pl.BlockSpec((SUB, 3), lambda i: (i, 0)),
-        ],
-        out_specs=(
-            pl.BlockSpec((2, SUB, width), lambda i: (0, i, 0)),
-            pl.BlockSpec((SUB, width), lambda i: (i, 0)),
-            pl.BlockSpec((SUB, width), lambda i: (i, 0)),
-        ),
-        compiler_params=pltpu.CompilerParams(vmem_limit_bytes=32 * 1024 * 1024),
+        compiler_params=pltpu.CompilerParams(vmem_limit_bytes=20 * 1024 * 1024),
         name="stencil",
     )(where_am_i, filt, filt, filt, south, north, coef)
     return uv, new_h, new_q

time: 93 us -> 82.8 us (0.89)
  local copies, waits for them, and re-layouts: 12 us -> 3.77 us
  Pallas kernels: 79 us -> 78 us
    unnamed x20 -> x8, local copies, waits for them, and re-layouts: 10.9 us -> 3.77 us
    pallas_call x1, Pallas kernels: 74.1 us -> 73.2 us  [per_device(): pl.pallas_call(functools.partial(filter_kernel, lat_size, lon_size, inner...]
where the time goes in v2:
time: 82.8 us; the launch traced here: 82.5 us
  Pallas kernels  78 us (94%)
  local copies, waits for them, and re-layouts  3.77 us (5%)
    pallas_call x1, Pallas kernels, per_device(): pl.pallas_call(functools.partial(filter_kernel, lat_size, lon_size, inner...  73.2 us
    pallas_call x1, Pallas kernels, per_device(): pl.pallas_call(functools.partial(stencil_kernel, steps, lat_size, ratio),...  4.88 us
    unnamed x8, local copies, waits for them, and re-layouts  3.77 us

profile of v2, /device:TPU:7, one launch (start us, length us, event | category | flops | bytes accessed | tf_op | source)
XLA Modules:
  0.0 82.5 jit_solution(13923816777098105718)
XLA Ops:
  0.6 0.0 copy-start.3
  0.6 73.2 %polar_filter.1 = (f32[4,64,2944]{2,1,0:T(8,128)}, f32[3,8,2944]{2,1,0:T(8,128)}, f32[3,8,2944]{2,1,0:T(8,128)}) custom-call(f32[2,64,2880]{2,1,0:T(8,128)} %winds.1, f32[64,2880]{1,0:T(8,128)} %thickness.1, f32[64,2880]{1,0:T(8,128)} %tracer.1, s32[64]{0:T(128)} %cutoff.1, f32[64]{0:T(128)} %damping.1, bf16[208,576]{1,0:T(8,128)(2,1)} %constant.21.clone.rest_0_, ...), custom_call_target="tpu_custom_call" | custom-call | flops 4000000000 | bytes 6029312 | tf_op jit(solution)/shard_map/polar_filter/pallas_call | solution.py:585
  73.8 0.0 copy-done.3
  73.8 0.0 copy-start
  73.8 1.8 %copy-done = f32[4,64,2944]{2,1,0:T(8,128)S(1)} copy-done((f32[4,64,2944]{2,1,0:T(8,128)S(1)}, f32[4,64,2944]{2,1,0:T(8,128)}, u32[]{:S(2)}) %copy-start) | copy-done | bytes 3014680
  75.7 0.0 copy-start.1
  75.7 1.0 %copy-done.1 = f32[3,8,2944]{2,1,0:T(8,128)S(1)} copy-done((f32[3,8,2944]{2,1,0:T(8,128)S(1)}, f32[3,8,2944]{2,1,0:T(8,128)}, u32[]{:S(2)}) %copy-start.1) | copy-done | bytes 282648
  76.6 0.0 copy-start.2
  76.6 1.0 %copy-done.2 = f32[3,8,2944]{2,1,0:T(8,128)S(1)} copy-done((f32[3,8,2944]{2,1,0:T(8,128)S(1)}, f32[3,8,2944]{2,1,0:T(8,128)}, u32[]{:S(2)}) %copy-start.2) | copy-done | bytes 282648
  77.6 4.9 %stencil.1 = (f32[2,64,2880]{2,1,0:T(8,128)}, f32[64,2880]{1,0:T(8,128)}, f32[64,2880]{1,0:T(8,128)}) custom-call(s32[1]{0:T(128)} %bitcast.where_ref, f32[4,64,2944]{2,1,0:T(8,128)S(1)} %copy-done, f32[4,64,2944]{2,1,0:T(8,128)S(1)} %copy-done, f32[4,64,2944]{2,1,0:T(8,128)S(1)} %copy-done, f32[3,8,2944]{2,1,0:T(8,128)S(1)} %copy-done.1, ...), custom_call_target="tpu_custom_call" | custom-call | tf_op jit(solution)/shard_map/stencil/pallas_call | solution.py:640
Async XLA Ops:
  0.6 73.2 %copy-start.3 = (f32[256,3]{1,0:T(8,128)S(1)}, f32[256,3]{1,0:T(8,128)}, u32[]{:S(2)}) copy-start(f32[256,3]{1,0:T(8,128)} %constant.28.clone.coef) | copy-start | bytes 9220
  73.8 1.9 %copy-start = (f32[4,64,2944]{2,1,0:T(8,128)S(1)}, f32[4,64,2944]{2,1,0:T(8,128)}, u32[]{:S(2)}) copy-start(f32[4,64,2944]{2,1,0:T(8,128)} %get-tuple-element.6.here.below.above) | copy-start | bytes 9043972
  75.7 1.0 %copy-start.1 = (f32[3,8,2944]{2,1,0:T(8,128)S(1)}, f32[3,8,2944]{2,1,0:T(8,128)}, u32[]{:S(2)}) copy-start(f32[3,8,2944]{2,1,0:T(8,128)} %get-tuple-element.7.south) | copy-start | bytes 847876
  76.6 1.0 %copy-start.2 = (f32[3,8,2944]{2,1,0:T(8,128)S(1)}, f32[3,8,2944]{2,1,0:T(8,128)}, u32[]{:S(2)}) copy-start(f32[3,8,2944]{2,1,0:T(8,128)} %get-tuple-element.8.north) | copy-start | bytes 847876

commit v3 on v2

--- a/solution.py
+++ b/solution.py
@@ -12,6 +12,7 @@
 LEV = 8
 LANES = 128
 SUB = 8
+UNIT = 4
 MESH = pl.DeviceIdType.MESH
 TABLES = 7
 EXACT = lax.Precision.HIGHEST
@@ -94,11 +95,13 @@
 
 
 def plan(lat_size, lon_size, row_count):
-    groups = row_count // SUB
-    split = lon_size // groups
+    groups = row_count // UNIT
+    turns = max(1, groups // lon_size)
+    span = groups // turns
+    split = lon_size // span
     planes = 1 if split == 4 else 2
-    slots = 4 // (planes * split)
-    return groups, split, planes, slots
+    each = 4 // (planes * split)
+    return groups, turns, span, split, planes, each
 
 
 def filter_kernel(
@@ -113,7 +116,7 @@
     *rest,
 ):
     table_in, rest = rest[:TABLES], rest[TABLES:]
-    (filt, south, north), rest = rest[:3], rest[3:]
+    filt, rest = rest[0], rest[1:]
     tables, rest = rest[:TABLES], rest[TABLES:]
     first, forward, backward, last, twiddle, wave, average = tables
     (
@@ -143,7 +146,8 @@
     ) = rest
     row_count, width = thickness.shape
     padded = filt.shape[-1]
-    groups, split, planes, slots = plan(lat_size, lon_size, row_count)
+    groups, turns, span, split, planes, each = plan(lat_size, lon_size, row_count)
+    slots = turns * each
     used = inner * LEV
     pieces = width // used
     outer = pieces * lon_size
@@ -158,8 +162,8 @@
     partner = band + bit - 2 * bit * lowbit
     home = jnp.where(is_polar, band, partner)
     my_plane = jnp.where(is_polar, 0, 1)
-    my_group = lax.rem(lon, groups)
-    my_split = lon // groups
+    my_place = lax.rem(lon, span)
+    my_split = lon // span
 
     def pair_of(b):
         return {b, b ^ bit} if planes == 2 else {b}
@@ -247,21 +251,36 @@
         pltpu.make_async_copy(dst, dst, rsem).wait()
 
     def forward_copies(slot, action):
-        for step in range(groups):
-            group = lax.rem(lon + step, groups)
+        turn = slot % turns
+        for step in range(span):
+            place = lax.rem(lon + step, span)
             for part in range(split):
                 for plane in reversed(range(planes)):
-                    target = part * groups + group
-                    field = (plane * split + part) * slots + slot
-                    rows = pl.ds(pl.multiple_of(group * SUB, SUB), SUB)
+                    target = part * span + place
+                    field = (plane * split + part) * each + slot // turns
                     action(
-                        own.at[field, rows, :],
+                        ext.at[1 + turn * span + place, field],
                         recv.at[slot, lon],
                         fwd_send.at[slot, plane, target],
                         fwd_recv.at[slot, lon],
                         partner if plane else band,
                         target,
                     )
+
+    def stage(field, turn):
+        def one(i, carry):
+            tile = turn * (span * UNIT // SUB) + i
+            rows = own[field, pl.ds(pl.multiple_of(tile * SUB, SUB), SUB), :]
+            for part in range(SUB // UNIT):
+                block = rows[part * UNIT : (part + 1) * UNIT]
+                ext[1 + tile * (SUB // UNIT) + part, field, :, :width] = block
+            return carry
+
+        lax.fori_loop(0, span * UNIT // SUB, one, 0)
+
+    def stage_slot(slot):
+        for lane in range(planes * split):
+            stage(lane * each + slot // turns, slot % turns)
 
     for load in loads:
         load.wait()
@@ -278,11 +297,16 @@
 
     @pl.when(is_polar)
     def _():
+        stage_slot(0)
         forward_copies(0, push)
-        for j in range(SUB):
-            row = my_group * SUB + j
-            prm[j : j + 1, :] = jnp.full((1, LANES), cutoff[row].astype(jnp.float32))
-            prm[SUB + j : SUB + j + 1, :] = jnp.full((1, LANES), damping[row])
+        for turn in range(turns):
+            for j in range(UNIT):
+                row = (turn * span + my_place) * UNIT + j
+                low, high = j, UNIT + j
+                prm[turn, low : low + 1] = jnp.full((1, LANES), cutoff[row].astype(jnp.float32))
+                prm[turn, high : high + 1] = jnp.full((1, LANES), damping[row])
+        for slot in range(1, slots):
+            stage_slot(slot)
         if planes == 2:
             param_copy().start()
 
@@ -298,11 +322,9 @@
         )
 
     def rim_copy(side, item):
-        rows = pl.ds(0, SUB) if side == 0 else pl.ds(row_count - SUB, SUB)
-        dst = north if side == 0 else south
         return pltpu.make_async_remote_copy(
-            src_ref=ext.at[item + 1, rows, :],
-            dst_ref=dst.at[item],
+            src_ref=ext.at[1 if side == 0 else groups, item + 1],
+            dst_ref=filt.at[groups + 1 if side == 0 else 0, item + 1],
             send_sem=rim_send.at[side, item],
             recv_sem=halo_recv.at[1 - side, item],
             device_id={"lat": band - 1 if side == 0 else band + 1, "lon": lon},
@@ -310,35 +332,37 @@
         )
 
     def keep_copy():
-        return pltpu.make_async_copy(ext, filt, filt_sem.at[0])
+        inner_groups = pl.ds(1, groups)
+        return pltpu.make_async_copy(ext.at[inner_groups], filt.at[inner_groups], filt_sem.at[0])
 
     @pl.when(jnp.logical_not(is_polar))
     def _():
+        for field in range(4):
+            for turn in range(turns):
+                stage(field, turn)
         for item, f in enumerate((0, 2, 3)):
-            edge[item, :, :LEV] = own[f, :, :LEV]
-            edge[item, :, LEV : 2 * LEV] = own[f, :, width - LEV :]
+            edge[item, :, :, :LEV] = ext[1 : groups + 1, f, :, :LEV]
+            edge[item, :, :, LEV : 2 * LEV] = ext[1 : groups + 1, f, :, width - LEV : width]
         edge_copy(0).start()
         edge_copy(1).start()
-        for f in range(4):
-            ext[f, :, :width] = own[f]
         edge_copy(0).wait()
         edge_copy(1).wait()
         for item, f in enumerate((0, 2, 3)):
-            ext[f, :, width : width + LEV] = edge_in[0, item, :, :LEV]
-            ext[f, :, padded - LEV :] = edge_in[1, item, :, LEV : 2 * LEV]
+            ext[1 : groups + 1, f, :, width : width + LEV] = edge_in[0, item, :, :, :LEV]
+            ext[1 : groups + 1, f, :, padded - LEV :] = edge_in[1, item, :, :, LEV : 2 * LEV]
         keep_copy().start()
         for side in range(2):
             for item in range(3):
                 rim_copy(side, item).start()
 
     def return_copies(slot, action):
-        field = (my_plane * split + my_split) * slots + slot
-        rows = pl.ds(pl.multiple_of(my_group * SUB, SUB), SUB)
+        field = (my_plane * split + my_split) * each + slot // turns
+        group = (slot % turns) * span + my_place
         for step in range(lon_size):
             target = lax.rem(lon + step, lon_size)
             action(
                 ret.at[slot, target],
-                filt.at[field, rows, :],
+                filt.at[1 + group, field],
                 ret_send.at[slot, target],
                 ret_recv.at[slot, my_plane, lon],
                 home,
@@ -347,7 +371,9 @@
         item = jnp.maximum(field - 1, 0)
         opposite = lon_size // 2
         for side in range(2):
-            at_edge = my_group == (0 if side == 0 else groups - 1)
+            if slot % turns != (0 if side == 0 else turns - 1):
+                continue
+            at_edge = group == (0 if side == 0 else groups - 1)
             at_pole = home == (0 if side == 0 else lat_size - 1)
             lat_to = home - 1 if side == 0 else home + 1
 
@@ -356,7 +382,7 @@
                 for target in range(lon_size):
                     action(
                         ret.at[slot, target],
-                        (north if side == 0 else south).at[item],
+                        filt.at[groups + 1 if side == 0 else 0, item + 1],
                         halo_send.at[slot, side, target],
                         halo_recv.at[1 - side, item],
                         lat_to,
@@ -368,14 +394,14 @@
                 for target in range(lon_size):
                     action(
                         ret.at[slot, target],
-                        (south if side == 0 else north).at[1],
+                        filt.at[0 if side == 0 else groups + 1, 2],
                         halo_send.at[slot, side, target],
                         halo_recv.at[side, 1],
                         home,
                         jnp.int32((target + opposite) % lon_size),
                     )
 
-    batch = 4
+    batch = UNIT
 
     def work(slot):
         for s in range(lon_size):
@@ -386,15 +412,15 @@
             for p in range(pieces):
                 piece = block[:, used * p : used * (p + 1)]
                 if used < LANES:
-                    blank = jnp.zeros((SUB, LANES - used), jnp.float32)
+                    blank = jnp.zeros((UNIT, LANES - used), jnp.float32)
                     piece = jnp.concatenate([piece, blank], axis=1)
-                spread[pl.ds(s * pieces + p, SUB, stride=outer), :] = piece
+                spread[pl.ds(s * pieces + p, UNIT, stride=outer), :] = piece
             return carry
 
         lax.fori_loop(0, lon_size, spread_sector, 0)
 
-        def some_rows(step, carry):
-            base = step * batch
+        def some_rows():
+            base = 0
             rows = [spread[pl.ds((base + j) * outer, outer), :] for j in range(batch)]
             sums = [jnp.sum(row, axis=0, keepdims=True) for row in rows] * (SUB // batch)
             mean = jnp.dot(
@@ -418,8 +444,8 @@
             inverse_k = 1.0 / jnp.maximum(k, 1.0)
             weighted = []
             for j in range(batch):
-                cut = prm[pl.ds(base + j, 1), :]
-                damp = prm[pl.ds(SUB + base + j, 1), :]
+                cut = prm[slot % turns, j : j + 1]
+                damp = prm[slot % turns, UNIT + j : UNIT + j + 1]
                 ratio = cut * inverse_k
                 factor = jnp.where(k > cut, damp * ratio * ratio, 1.0)
                 weighted.append(
@@ -437,18 +463,17 @@
             for j in range(batch):
                 piece = out[:, j * LANES : (j + 1) * LANES] + means[j]
                 done[pl.ds((base + j) * outer, outer), :] = piece
-            return carry
-
-        lax.fori_loop(0, SUB // batch, some_rows, 0)
+
+        some_rows()
 
         def gather_sector(s, carry):
             for p in range(pieces):
-                piece = done[pl.ds(s * pieces + p, SUB, stride=outer), :]
+                piece = done[pl.ds(s * pieces + p, UNIT, stride=outer), :]
                 ret[slot, s, :, used * p : used * (p + 1)] = piece[:, :used]
             east = lax.rem(s + 1, lon_size) * pieces
             west = lax.rem(s + lon_size - 1, lon_size) * pieces + pieces - 1
-            ret[slot, s, :, width : width + LEV] = done[pl.ds(east, SUB, stride=outer), :][:, :LEV]
-            ret[slot, s, :, padded - LEV :] = done[pl.ds(west, SUB, stride=outer), :][
+            ret[slot, s, :, width : width + LEV] = done[pl.ds(east, UNIT, stride=outer), :][:, :LEV]
+            ret[slot, s, :, padded - LEV :] = done[pl.ds(west, UNIT, stride=outer), :][
                 :, used - LEV : used
             ]
             return carry
@@ -490,11 +515,9 @@
         for slot in range(slots):
             for plane in range(planes):
                 for source in range(lon_size):
-                    field = (plane * split + source // groups) * slots + slot
-                    row = (source % groups) * SUB
-                    arrived(
-                        filt.at[field, pl.ds(row, SUB), :], ret_recv.at[slot, plane, source]
-                    )
+                    field = (plane * split + source // span) * each + slot // turns
+                    group = (slot % turns) * span + source % span
+                    arrived(filt.at[1 + group, field], ret_recv.at[slot, plane, source])
 
     @pl.when(jnp.logical_not(is_polar))
     def _():
@@ -503,39 +526,36 @@
             for item in range(3):
                 rim_copy(side, item).wait_send()
 
-    for side, rim in enumerate((south, north)):
+    for side, rim in enumerate((0, groups + 1)):
         at_pole = band == (0 if side == 0 else lat_size - 1)
-        arrived(rim.at[1], halo_recv.at[side, 1])
+        arrived(filt.at[rim, 2], halo_recv.at[side, 1])
 
         @pl.when(jnp.logical_not(at_pole))
         def _():
-            arrived(rim.at[0], halo_recv.at[side, 0])
-            arrived(rim.at[2], halo_recv.at[side, 2])
-
-
-def stencil_kernel(
-    steps, lat_size, ratio, where_ref, here, below, above, south, north, coef, uv, new_h, new_q
-):
+            arrived(filt.at[rim, 1], halo_recv.at[side, 0])
+            arrived(filt.at[rim, 3], halo_recv.at[side, 2])
+
+
+def stencil_kernel(steps, lat_size, ratio, where_ref, below, *rest):
+    parts = SUB // UNIT
+    here, above, coef, uv, new_h, new_q = rest[:parts], *rest[parts:]
     step = pl.program_id(0)
     band = where_ref[0]
     width = new_h.shape[-1]
-    padded = here.shape[-1]
-    first, final = step == 0, step == steps - 1
-    low_pole = first & (band == 0)
-    high_pole = final & (band == lat_size - 1)
-    u, v, h, q = here[0], here[1], here[2], here[3]
-
-    def south_of(x, item):
-        row = jnp.where(first, south[item, SUB - 1 : SUB, :], below[item + 1, SUB - 1 : SUB, :])
-        pole = south[1, 0:1, :] if item == 1 else jnp.zeros_like(row)
-        row = jnp.where(low_pole, pole, row)
-        return jnp.concatenate([row, x[: SUB - 1]], axis=0)
-
-    def north_of(x, item):
-        row = jnp.where(final, north[item, 0:1, :], above[item + 1, 0:1, :])
-        pole = north[1, SUB - 1 : SUB, :] if item == 1 else jnp.zeros_like(row)
-        row = jnp.where(high_pole, pole, row)
-        return jnp.concatenate([x[1:], row], axis=0)
+    padded = below.shape[-1]
+    low_pole = (step == 0) & (band == 0)
+    high_pole = (step == steps - 1) & (band == lat_size - 1)
+    u, v, h, q = [jnp.concatenate([part[0, f] for part in here], axis=0) for f in range(4)]
+
+    def south_of(x, f):
+        row = below[0, f, UNIT - 1 : UNIT, :]
+        pole = below[0, f, 0:1, :] if f == 2 else jnp.zeros_like(row)
+        return jnp.concatenate([jnp.where(low_pole, pole, row), x[: SUB - 1]], axis=0)
+
+    def north_of(x, f):
+        row = above[0, f, 0:1, :]
+        pole = above[0, f, UNIT - 1 : UNIT, :] if f == 2 else jnp.zeros_like(row)
+        return jnp.concatenate([x[1:], jnp.where(high_pole, pole, row)], axis=0)
 
     def east_of(x):
         return pltpu.roll(x, padded - LEV, 1)
@@ -546,15 +566,15 @@
     inv_c = coef[:, 0:1]
     face_s = coef[:, 1:2]
     face_n = coef[:, 2:3]
-    he, hs, hn = east_of(h), south_of(h, 1), north_of(h, 1)
+    he, hs, hn = east_of(h), south_of(h, 2), north_of(h, 2)
     hw = west_of(h)
     wind = 0.25 * (u + east_of(u))
     fx = wind * (h + he)
     gx = wind * (q + east_of(q))
-    wind_s = face_s * (south_of(v, 0) + v)
-    wind_n = face_n * (v + north_of(v, 0))
+    wind_s = face_s * (south_of(v, 1) + v)
+    wind_n = face_n * (v + north_of(v, 1))
     fy = wind_n * (h + hn) - wind_s * (hs + h)
-    gy = wind_n * (q + north_of(q, 2)) - wind_s * (south_of(q, 2) + q)
+    gy = wind_n * (q + north_of(q, 3)) - wind_s * (south_of(q, 3) + q)
     out_h = h - ((fx - west_of(fx)) + fy) * inv_c
     out_q = q - ((gx - west_of(gx)) + gy) * inv_c
     out_u = u - (he - hw) * (0.5 * inv_c)
@@ -576,32 +596,29 @@
     inner = inner_length(columns)
     outer = length // inner
     padded = round_up(width + 2 * LEV, LANES)
-    groups, split, planes, slots = plan(lat_size, lon_size, row_count)
+    groups, turns, span, split, planes, each = plan(lat_size, lon_size, row_count)
+    slots = turns * each
     tables = [jnp.asarray(t) for t in dft_tables(length, inner)]
     vmem_spec = pl.BlockSpec(memory_space=pltpu.VMEM)
     hbm_spec = pl.BlockSpec(memory_space=pltpu.HBM)
     smem_spec = pl.BlockSpec(memory_space=pltpu.SMEM)
     f32 = jnp.float32
-    filt, south, north = pl.pallas_call(
+    filt = pl.pallas_call(
         functools.partial(filter_kernel, lat_size, lon_size, inner),
-        out_shape=(
-            jax.ShapeDtypeStruct((4, row_count, padded), f32),
-            jax.ShapeDtypeStruct((3, SUB, padded), f32),
-            jax.ShapeDtypeStruct((3, SUB, padded), f32),
-        ),
+        out_shape=jax.ShapeDtypeStruct((groups + 2, 4, UNIT, padded), f32),
         in_specs=[hbm_spec] * 3 + [smem_spec] * 2 + [hbm_spec] * TABLES,
-        out_specs=(vmem_spec,) * 3,
+        out_specs=vmem_spec,
         scratch_shapes=[pltpu.VMEM(t.shape, t.dtype) for t in tables]
         + [
-            pltpu.VMEM((slots, lon_size, SUB, width), f32),
-            pltpu.VMEM((SUB * outer, LANES), f32),
-            pltpu.VMEM((SUB * outer, LANES), f32),
-            pltpu.VMEM((slots, lon_size, SUB, padded), f32),
+            pltpu.VMEM((slots, lon_size, UNIT, padded), f32),
+            pltpu.VMEM((UNIT * outer, LANES), f32),
+            pltpu.VMEM((UNIT * outer, LANES), f32),
+            pltpu.VMEM((slots, lon_size, UNIT, padded), f32),
             pltpu.VMEM((4, row_count, width), f32),
-            pltpu.VMEM((4, row_count, padded), f32),
-            pltpu.VMEM((3, row_count, LANES), f32),
-            pltpu.VMEM((2, 3, row_count, LANES), f32),
-            pltpu.VMEM((2 * SUB, LANES), f32),
+            pltpu.VMEM((groups + 2, 4, UNIT, padded), f32),
+            pltpu.VMEM((3, groups, UNIT, LANES), f32),
+            pltpu.VMEM((2, 3, groups, UNIT, LANES), f32),
+            pltpu.VMEM((turns, 2 * UNIT, LANES), f32),
             pltpu.SemaphoreType.DMA((slots, planes, lon_size)),
             pltpu.SemaphoreType.DMA((slots, lon_size)),
             pltpu.SemaphoreType.DMA((slots, lon_size)),
@@ -635,19 +652,21 @@
     coef = jnp.asarray(np.stack([1.0 / centers, faces[:-1], faces[1:]], axis=1), f32)
     steps = row_count // SUB
     where_am_i = band.astype(jnp.int32).reshape(1)
-    block = (4, SUB, padded)
-    whole = (3, SUB, padded)
+    block = (1, 4, UNIT, padded)
+
+    def block_of(part, i, b):
+        return (i * (SUB // UNIT) + part, 0, 0, 0)
+
     uv, new_h, new_q = pl.pallas_call(
         functools.partial(stencil_kernel, steps, lat_size, ratio),
         grid_spec=pltpu.PrefetchScalarGridSpec(
             num_scalar_prefetch=1,
             grid=(steps,),
             in_specs=[
-                pl.BlockSpec(block, lambda i, b: (0, i, 0)),
-                pl.BlockSpec(block, lambda i, b: (0, jnp.maximum(i - 1, 0), 0)),
-                pl.BlockSpec(block, lambda i, b: (0, jnp.minimum(i + 1, steps - 1), 0)),
-                pl.BlockSpec(whole, lambda i, b: (0, 0, 0)),
-                pl.BlockSpec(whole, lambda i, b: (0, 0, 0)),
+                pl.BlockSpec(block, functools.partial(block_of, part))
+                for part in range(SUB // UNIT + 2)
+            ]
+            + [
                 pl.BlockSpec((SUB, 3), lambda i, b: (b[0] * steps + i, 0)),
             ],
             out_specs=(
@@ -663,7 +682,7 @@
         ),
         compiler_params=pltpu.CompilerParams(vmem_limit_bytes=20 * 1024 * 1024),
         name="stencil",
-    )(where_am_i, filt, filt, filt, south, north, coef)
+    )(where_am_i, *[filt] * (SUB // UNIT + 2), coef)
     return uv, new_h, new_q
 
 

time: 82.8 us -> 74.1 us (0.89)
  Pallas kernels: 78 us -> 70.7 us
  local copies, waits for them, and re-layouts: 3.77 us -> 1.96 us
    pallas_call x1, Pallas kernels: 73.2 us -> 66.2 us  [per_device(): pl.pallas_call(functools.partial(filter_kernel, lat_size, lon_size, inner...]
    unnamed x8 -> x4, local copies, waits for them, and re-layouts: 3.77 us -> 1.96 us
where the time goes in v3:
time: 74.1 us; the launch traced here: 73.3 us
  Pallas kernels  70.7 us (95%)
  local copies, waits for them, and re-layouts  1.96 us (3%)
    pallas_call x1, Pallas kernels, per_device(): pl.pallas_call(functools.partial(filter_kernel, lat_size, lon_size, inner...  66.2 us
    pallas_call x1, Pallas kernels, per_device(): pl.pallas_call(functools.partial(stencil_kernel, steps, lat_size, ratio),...  4.41 us
    unnamed x4, local copies, waits for them, and re-layouts  1.96 us

profile of v3, /device:TPU:7, one launch (start us, length us, event | category | flops | bytes accessed | tf_op | source)
XLA Modules:
  0.0 73.3 jit_solution(1822703343203083229)
XLA Ops:
  0.6 0.0 copy-start.1
  0.6 66.2 %polar_filter.1.below.rest_0_.rest_1_.rest_2_ = f32[18,4,4,2944]{3,2,1,0:T(4,128)} custom-call(f32[2,64,2880]{2,1,0:T(8,128)} %winds.1, f32[64,2880]{1,0:T(8,128)} %thickness.1, f32[64,2880]{1,0:T(8,128)} %tracer.1, s32[64]{0:T(128)} %cutoff.1, f32[64]{0:T(128)} %damping.1, bf16[208,576]{1,0:T(8,128)(2,1)} %constant.21.clone.rest_0_, ...), custom_call_target="tpu_custom_call" | custom-call | flops 4000000000 | bytes 6029312 | tf_op jit(solution)/shard_map/polar_filter/pallas_call | solution.py:606
  66.9 0.0 copy-done.1
  66.9 0.0 copy-start
  66.9 2.0 %copy-done = f32[18,4,4,2944]{3,2,1,0:T(4,128)S(1)} copy-done((f32[18,4,4,2944]{3,2,1,0:T(4,128)S(1)}, f32[18,4,4,2944]{3,2,1,0:T(4,128)}, u32[]{:S(2)}) %copy-start) | copy-done | bytes 3391512
  68.9 4.4 %stencil.1 = (f32[2,64,2880]{2,1,0:T(8,128)}, f32[64,2880]{1,0:T(8,128)}, f32[64,2880]{1,0:T(8,128)}) custom-call(s32[1]{0:T(128)} %bitcast.where_ref, f32[18,4,4,2944]{3,2,1,0:T(4,128)S(1)} %copy-done, f32[18,4,4,2944]{3,2,1,0:T(4,128)S(1)} %copy-done, f32[18,4,4,2944]{3,2,1,0:T(4,128)S(1)} %copy-done, f32[18,4,4,2944]{3,2,1,0:T(4,128)S(1)} %copy-done, ...), custom_call_target="tpu_custom_call" | custom-call | tf_op jit(solution)/shard_map/stencil/pallas_call | solution.py:660
Async XLA Ops:
  0.6 66.3 %copy-start.1 = (f32[256,3]{1,0:T(8,128)S(1)}, f32[256,3]{1,0:T(8,128)}, u32[]{:S(2)}) copy-start(f32[256,3]{1,0:T(8,128)} %constant.28.clone.rest_3_) | copy-start | bytes 9220
  66.9 2.0 %copy-start = (f32[18,4,4,2944]{3,2,1,0:T(4,128)S(1)}, f32[18,4,4,2944]{3,2,1,0:T(4,128)}, u32[]{:S(2)}) copy-start(f32[18,4,4,2944]{3,2,1,0:T(4,128)} %polar_filter.1.below.rest_0_.rest_1_.rest_2_) | copy-start | bytes 10174468

commit v4 on v3

--- a/solution.py
+++ b/solution.py
@@ -99,9 +99,11 @@
     turns = max(1, groups // lon_size)
     span = groups // turns
     split = lon_size // span
-    planes = 1 if split == 4 else 2
-    each = 4 // (planes * split)
-    return groups, turns, span, split, planes, each
+    jobs = []
+    for field in range(0, 4, split):
+        jobs += [(tuple(range(field, field + split)), turn) for turn in range(turns)]
+    lent = 3 * len(jobs) // 8 if split == 1 else len(jobs) // 2
+    return groups, turns, span, split, jobs[: len(jobs) - lent], jobs[len(jobs) - lent :]
 
 
 def filter_kernel(
@@ -121,7 +123,8 @@
     first, forward, backward, last, twiddle, wave, average = tables
     (
 
-        recv,
+        relay,
+    recv,
     spread,
     done,
     ret,
@@ -130,6 +133,8 @@
     edge,
     edge_in,
     prm,
+    relay_send,
+    relay_recv,
     fwd_send,
     fwd_recv,
     ret_send,
@@ -146,8 +151,8 @@
     ) = rest
     row_count, width = thickness.shape
     padded = filt.shape[-1]
-    groups, turns, span, split, planes, each = plan(lat_size, lon_size, row_count)
-    slots = turns * each
+    groups, turns, span, split, kept_jobs, lent_jobs = plan(lat_size, lon_size, row_count)
+    planes = 2 if lent_jobs else 1
     used = inner * LEV
     pieces = width // used
     outer = pieces * lon_size
@@ -250,22 +255,53 @@
     def arrived(dst, rsem):
         pltpu.make_async_copy(dst, dst, rsem).wait()
 
-    def forward_copies(slot, action):
-        turn = slot % turns
+    def own_copies(slot, action):
+        fields, turn = kept_jobs[slot]
         for step in range(span):
             place = lax.rem(lon + step, span)
             for part in range(split):
-                for plane in reversed(range(planes)):
-                    target = part * span + place
-                    field = (plane * split + part) * each + slot // turns
-                    action(
-                        ext.at[1 + turn * span + place, field],
-                        recv.at[slot, lon],
-                        fwd_send.at[slot, plane, target],
-                        fwd_recv.at[slot, lon],
-                        partner if plane else band,
-                        target,
-                    )
+                target = part * span + place
+                action(
+                    ext.at[1 + turn * span + place, fields[part]],
+                    recv.at[slot, lon],
+                    fwd_send.at[slot, target],
+                    fwd_recv.at[slot, lon],
+                    band,
+                    target,
+                )
+
+    def relay_copies(slot):
+        fields, turn = lent_jobs[slot]
+        return [
+            pltpu.make_async_remote_copy(
+                src_ref=ext.at[pl.ds(1 + turn * span, span), fields[part]],
+                dst_ref=relay.at[slot, part],
+                send_sem=relay_send.at[slot, part],
+                recv_sem=relay_recv.at[slot, part],
+                device_id={"lat": partner, "lon": lon},
+                device_id_type=MESH,
+            )
+            for part in range(split)
+        ]
+
+    def spread_copies(slot, action):
+        for step in range(span):
+            place = lax.rem(lon + step, span)
+            for part in range(split):
+                target = part * span + place
+                action(
+                    relay.at[slot, part, place],
+                    recv.at[slot, lon],
+                    fwd_send.at[slot, target],
+                    fwd_recv.at[slot, lon],
+                    band,
+                    target,
+                )
+
+    def relayed(slot):
+        for copy in relay_copies(slot):
+            copy.wait_recv()
+        spread_copies(slot, push)
 
     def stage(field, turn):
         def one(i, carry):
@@ -278,9 +314,9 @@
 
         lax.fori_loop(0, span * UNIT // SUB, one, 0)
 
-    def stage_slot(slot):
-        for lane in range(planes * split):
-            stage(lane * each + slot // turns, slot % turns)
+    def stage_job(job):
+        for field in job[0]:
+            stage(field, job[1])
 
     for load in loads:
         load.wait()
@@ -297,16 +333,20 @@
 
     @pl.when(is_polar)
     def _():
-        stage_slot(0)
-        forward_copies(0, push)
+        for job in lent_jobs[:1]:
+            stage_job(job)
+            for copy in relay_copies(0):
+                copy.start()
+        stage_job(kept_jobs[0])
+        own_copies(0, push)
         for turn in range(turns):
             for j in range(UNIT):
                 row = (turn * span + my_place) * UNIT + j
                 low, high = j, UNIT + j
                 prm[turn, low : low + 1] = jnp.full((1, LANES), cutoff[row].astype(jnp.float32))
                 prm[turn, high : high + 1] = jnp.full((1, LANES), damping[row])
-        for slot in range(1, slots):
-            stage_slot(slot)
+        for job in kept_jobs[1:] + lent_jobs[1:]:
+            stage_job(job)
         if planes == 2:
             param_copy().start()
 
@@ -355,9 +395,24 @@
             for item in range(3):
                 rim_copy(side, item).start()
 
+    def job_of(slot):
+        def pick(jobs):
+            fields, turn = jobs[min(slot, len(jobs) - 1)]
+            field = jnp.int32(fields[0])
+            for part in range(1, split):
+                field = jnp.where(my_split == part, fields[part], field)
+            return field, jnp.int32(turn)
+
+        field, turn = pick(kept_jobs)
+        if lent_jobs:
+            lent_field, lent_turn = pick(lent_jobs)
+            field = jnp.where(is_polar, field, lent_field)
+            turn = jnp.where(is_polar, turn, lent_turn)
+        return field, turn
+
     def return_copies(slot, action):
-        field = (my_plane * split + my_split) * each + slot // turns
-        group = (slot % turns) * span + my_place
+        field, turn = job_of(slot)
+        group = turn * span + my_place
         for step in range(lon_size):
             target = lax.rem(lon + step, lon_size)
             action(
@@ -371,8 +426,6 @@
         item = jnp.maximum(field - 1, 0)
         opposite = lon_size // 2
         for side in range(2):
-            if slot % turns != (0 if side == 0 else turns - 1):
-                continue
             at_edge = group == (0 if side == 0 else groups - 1)
             at_pole = home == (0 if side == 0 else lat_size - 1)
             lat_to = home - 1 if side == 0 else home + 1
@@ -404,6 +457,7 @@
     batch = UNIT
 
     def work(slot):
+        _, turn = job_of(slot)
         for s in range(lon_size):
             arrived(recv.at[slot, s], fwd_recv.at[slot, s])
 
@@ -444,8 +498,8 @@
             inverse_k = 1.0 / jnp.maximum(k, 1.0)
             weighted = []
             for j in range(batch):
-                cut = prm[slot % turns, j : j + 1]
-                damp = prm[slot % turns, UNIT + j : UNIT + j + 1]
+                cut = prm[turn, j : j + 1]
+                damp = prm[turn, UNIT + j : UNIT + j + 1]
                 ratio = cut * inverse_k
                 factor = jnp.where(k > cut, damp * ratio * ratio, 1.0)
                 weighted.append(
@@ -481,43 +535,70 @@
         lax.fori_loop(0, lon_size, gather_sector, 0)
         return_copies(slot, push)
 
-    def all_work():
-        for slot in range(slots):
-            if slot + 1 < slots:
-
-                @pl.when(is_polar)
-                def _():
-                    forward_copies(slot, sent)
-                    forward_copies(slot + 1, push)
-
-            work(slot)
-        for slot in range(slots):
-            return_copies(slot, sent)
-
     for load in table_loads:
         load.wait()
 
-    if planes == 2:
+    if lent_jobs:
 
         @pl.when(jnp.logical_not(is_polar))
         def _():
             param_copy().wait_recv()
-
-        all_work()
-    else:
-        pl.when(is_polar)(all_work)
+            relayed(0)
+
+    kept_count, lent_count = len(kept_jobs), len(lent_jobs)
+    for slot in range(max(kept_count, lent_count)):
+
+        @pl.when(is_polar)
+        def _():
+            if slot + 1 < kept_count:
+                own_copies(slot, sent)
+                own_copies(slot + 1, push)
+            if slot >= 2 and slot < lent_count:
+                for copy in relay_copies(slot - 2):
+                    copy.wait_send()
+                for copy in relay_copies(slot):
+                    copy.start()
+            if slot == 0 and lent_count > 1:
+                for copy in relay_copies(1):
+                    copy.start()
+
+        if slot + 1 < lent_count:
+
+            @pl.when(jnp.logical_not(is_polar))
+            def _():
+                relayed(slot + 1)
+
+        if slot < kept_count and slot < lent_count:
+            work(slot)
+        elif slot < kept_count:
+            pl.when(is_polar)(functools.partial(work, slot))
+        else:
+            pl.when(jnp.logical_not(is_polar))(functools.partial(work, slot))
 
     @pl.when(is_polar)
     def _():
-        if planes == 2:
+        if lent_jobs:
             param_copy().wait_send()
-        forward_copies(slots - 1, sent)
-        for slot in range(slots):
-            for plane in range(planes):
+            for slot in range(max(0, lent_count - 2), lent_count):
+                for copy in relay_copies(slot):
+                    copy.wait_send()
+        own_copies(kept_count - 1, sent)
+        for slot in range(kept_count):
+            return_copies(slot, sent)
+        for plane, jobs in enumerate((kept_jobs, lent_jobs)):
+            for slot, (fields, turn) in enumerate(jobs):
                 for source in range(lon_size):
-                    field = (plane * split + source // span) * each + slot // turns
-                    group = (slot % turns) * span + source % span
+                    group = turn * span + source % span
+                    field = fields[source // span]
                     arrived(filt.at[1 + group, field], ret_recv.at[slot, plane, source])
+
+    if lent_jobs:
+
+        @pl.when(jnp.logical_not(is_polar))
+        def _():
+            for slot in range(lent_count):
+                spread_copies(slot, sent)
+                return_copies(slot, sent)
 
     @pl.when(jnp.logical_not(is_polar))
     def _():
@@ -596,8 +677,9 @@
     inner = inner_length(columns)
     outer = length // inner
     padded = round_up(width + 2 * LEV, LANES)
-    groups, turns, span, split, planes, each = plan(lat_size, lon_size, row_count)
-    slots = turns * each
+    groups, turns, span, split, kept_jobs, lent_jobs = plan(lat_size, lon_size, row_count)
+    slots = max(len(kept_jobs), len(lent_jobs))
+    relays = max(1, len(lent_jobs))
     tables = [jnp.asarray(t) for t in dft_tables(length, inner)]
     vmem_spec = pl.BlockSpec(memory_space=pltpu.VMEM)
     hbm_spec = pl.BlockSpec(memory_space=pltpu.HBM)
@@ -610,6 +692,7 @@
         out_specs=vmem_spec,
         scratch_shapes=[pltpu.VMEM(t.shape, t.dtype) for t in tables]
         + [
+            pltpu.VMEM((relays, split, span, UNIT, padded), f32),
             pltpu.VMEM((slots, lon_size, UNIT, padded), f32),
             pltpu.VMEM((UNIT * outer, LANES), f32),
             pltpu.VMEM((UNIT * outer, LANES), f32),
@@ -619,7 +702,9 @@
             pltpu.VMEM((3, groups, UNIT, LANES), f32),
             pltpu.VMEM((2, 3, groups, UNIT, LANES), f32),
             pltpu.VMEM((turns, 2 * UNIT, LANES), f32),
-            pltpu.SemaphoreType.DMA((slots, planes, lon_size)),
+            pltpu.SemaphoreType.DMA((relays, split)),
+            pltpu.SemaphoreType.DMA((relays, split)),
+            pltpu.SemaphoreType.DMA((slots, lon_size)),
             pltpu.SemaphoreType.DMA((slots, lon_size)),
             pltpu.SemaphoreType.DMA((slots, lon_size)),
             pltpu.SemaphoreType.DMA((slots, 2, lon_size)),

time: 74.1 us -> 75.5 us (1.019)
  Pallas kernels: 70.7 us -> 71.6 us
    pallas_call x1, Pallas kernels: 66.2 us -> 67.2 us  [per_device(): pl.pallas_call(functools.partial(filter_kernel, lat_size, lon_size, inner...]
where the time goes in v4:
time: 75.5 us; the launch traced here: 74.3 us
  Pallas kernels  71.6 us (95%)
  local copies, waits for them, and re-layouts  1.96 us (3%)
    pallas_call x1, Pallas kernels, per_device(): pl.pallas_call(functools.partial(filter_kernel, lat_size, lon_size, inner...  67.2 us
    pallas_call x1, Pallas kernels, per_device(): pl.pallas_call(functools.partial(stencil_kernel, steps, lat_size, ratio),...  4.41 us
    unnamed x4, local copies, waits for them, and re-layouts  1.96 us

profile of v4, /device:TPU:7, one launch (start us, length us, event | category | flops | bytes accessed | tf_op | source)
XLA Modules:
  0.0 74.3 jit_solution(2379160996098435977)
XLA Ops:
  0.6 0.0 copy-start.1
  0.6 67.2 %polar_filter.1.below.rest_0_.rest_1_.rest_2_ = f32[18,4,4,2944]{3,2,1,0:T(4,128)} custom-call(f32[2,64,2880]{2,1,0:T(8,128)} %winds.1, f32[64,2880]{1,0:T(8,128)} %thickness.1, f32[64,2880]{1,0:T(8,128)} %tracer.1, s32[64]{0:T(128)} %cutoff.1, f32[64]{0:T(128)} %damping.1, bf16[208,576]{1,0:T(8,128)(2,1)} %constant.21.clone.rest_0_, ...), custom_call_target="tpu_custom_call" | custom-call | flops 4000000000 | bytes 6029312 | tf_op jit(solution)/shard_map/polar_filter/pallas_call | solution.py:688
  67.9 0.0 copy-done.1
  67.9 0.0 copy-start
  67.9 2.0 %copy-done = f32[18,4,4,2944]{3,2,1,0:T(4,128)S(1)} copy-done((f32[18,4,4,2944]{3,2,1,0:T(4,128)S(1)}, f32[18,4,4,2944]{3,2,1,0:T(4,128)}, u32[]{:S(2)}) %copy-start) | copy-done | bytes 3391512
  69.8 4.4 %stencil.1 = (f32[2,64,2880]{2,1,0:T(8,128)}, f32[64,2880]{1,0:T(8,128)}, f32[64,2880]{1,0:T(8,128)}) custom-call(s32[1]{0:T(128)} %bitcast.where_ref, f32[18,4,4,2944]{3,2,1,0:T(4,128)S(1)} %copy-done, f32[18,4,4,2944]{3,2,1,0:T(4,128)S(1)} %copy-done, f32[18,4,4,2944]{3,2,1,0:T(4,128)S(1)} %copy-done, f32[18,4,4,2944]{3,2,1,0:T(4,128)S(1)} %copy-done, ...), custom_call_target="tpu_custom_call" | custom-call | tf_op jit(solution)/shard_map/stencil/pallas_call | solution.py:745
Async XLA Ops:
  0.6 67.2 %copy-start.1 = (f32[256,3]{1,0:T(8,128)S(1)}, f32[256,3]{1,0:T(8,128)}, u32[]{:S(2)}) copy-start(f32[256,3]{1,0:T(8,128)} %constant.28.clone.rest_3_) | copy-start | bytes 9220
  67.9 2.0 %copy-start = (f32[18,4,4,2944]{3,2,1,0:T(4,128)S(1)}, f32[18,4,4,2944]{3,2,1,0:T(4,128)}, u32[]{:S(2)}) copy-start(f32[18,4,4,2944]{3,2,1,0:T(4,128)} %polar_filter.1.below.rest_0_.rest_1_.rest_2_) | copy-start | bytes 10174468

commit v5 on v4

--- a/solution.py
+++ b/solution.py
@@ -15,15 +15,10 @@
 UNIT = 4
 MESH = pl.DeviceIdType.MESH
 TABLES = 7
-EXACT = lax.Precision.HIGHEST
 
 
 def round_up(value, step):
     return -(-value // step) * step
-
-
-def inner_length(columns):
-    return max(a for a in range(1, LANES // LEV + 1) if columns % a == 0)
 
 
 def halves(x):
@@ -45,18 +40,19 @@
 
 def dft_tables(length, inner):
     outer = length // inner
+    depth = round_up(outer, 2 * SUB)
     half = outer // 2 + 1
     kept = round_up(half, SUB)
     p = np.arange(outer)
     k1 = np.arange(half)
     angle = 2.0 * np.pi * ((p[None, :] * k1[:, None]) % outer) / outer
-    first = np.zeros((2 * kept, outer))
-    first[:half] = np.cos(angle)
-    first[kept : kept + half] = -np.sin(angle)
+    first = np.zeros((2 * kept, depth))
+    first[:half, :outer] = np.cos(angle)
+    first[kept : kept + half, :outer] = -np.sin(angle)
     twice = np.where((k1 == 0) | (2 * k1 == outer), 1.0, 2.0)[:, None] / length
-    last = np.zeros((outer, 2 * kept))
-    last[:, :half] = (twice * np.cos(angle)).T
-    last[:, kept : kept + half] = (-twice * np.sin(angle)).T
+    last = np.zeros((depth, 2 * kept))
+    last[:outer, :half] = (twice * np.cos(angle)).T
+    last[:outer, kept : kept + half] = (-twice * np.sin(angle)).T
     a = np.arange(inner)
     turn = 2.0 * np.pi * ((k1[:, None] * a[None, :]) % length) / length
     twiddle = np.zeros((2, kept, LANES))
@@ -109,7 +105,6 @@
 def filter_kernel(
     lat_size,
     lon_size,
-    inner,
     winds,
     thickness,
     tracer,
@@ -153,9 +148,10 @@
     padded = filt.shape[-1]
     groups, turns, span, split, kept_jobs, lent_jobs = plan(lat_size, lon_size, row_count)
     planes = 2 if lent_jobs else 1
-    used = inner * LEV
-    pieces = width // used
-    outer = pieces * lon_size
+    outer = width * lon_size // LANES
+    depth = first.shape[1] // 3
+    period = math.lcm(width, LANES)
+    near_sectors, near_tiles = period // width, period // LANES
     kept = wave.shape[0]
     quarter = lat_size // 4
     bit = 1 << (lat_size.bit_length() - 3)
@@ -318,6 +314,7 @@
         for field in job[0]:
             stage(field, job[1])
 
+    spread[...] = jnp.zeros_like(spread)
     for load in loads:
         load.wait()
 
@@ -461,26 +458,26 @@
         for s in range(lon_size):
             arrived(recv.at[slot, s], fwd_recv.at[slot, s])
 
-        def spread_sector(s, carry):
-            block = recv[slot, s]
-            for p in range(pieces):
-                piece = block[:, used * p : used * (p + 1)]
-                if used < LANES:
-                    blank = jnp.zeros((UNIT, LANES - used), jnp.float32)
-                    piece = jnp.concatenate([piece, blank], axis=1)
-                spread[pl.ds(s * pieces + p, UNIT, stride=outer), :] = piece
+        def spread_period(m, carry):
+            for t in range(near_tiles):
+                source, lane = divmod(t * LANES, width)
+                take = min(LANES, width - lane)
+                tile = recv[slot, m * near_sectors + source, :, lane : lane + take]
+                if take < LANES:
+                    more = recv[slot, m * near_sectors + source + 1, :, : LANES - take]
+                    tile = jnp.concatenate([tile, more], axis=1)
+                spread[pl.ds(m * near_tiles + t, UNIT, stride=depth), :] = tile
             return carry
 
-        lax.fori_loop(0, lon_size, spread_sector, 0)
+        lax.fori_loop(0, lon_size // near_sectors, spread_period, 0)
 
         def some_rows():
             base = 0
-            rows = [spread[pl.ds((base + j) * outer, outer), :] for j in range(batch)]
+            rows = [spread[pl.ds((base + j) * depth, depth), :] for j in range(batch)]
             sums = [jnp.sum(row, axis=0, keepdims=True) for row in rows] * (SUB // batch)
             mean = jnp.dot(
                 jnp.concatenate(sums, axis=0),
                 average[...],
-                precision=EXACT,
                 preferred_element_type=jnp.float32,
             )
             means = [mean[j : j + 1] for j in range(batch)]
@@ -516,23 +513,34 @@
             out = left_dot(last, u)
             for j in range(batch):
                 piece = out[:, j * LANES : (j + 1) * LANES] + means[j]
-                done[pl.ds((base + j) * outer, outer), :] = piece
+                done[pl.ds((base + j) * depth, depth), :] = piece
 
         some_rows()
 
-        def gather_sector(s, carry):
-            for p in range(pieces):
-                piece = done[pl.ds(s * pieces + p, UNIT, stride=outer), :]
-                ret[slot, s, :, used * p : used * (p + 1)] = piece[:, :used]
-            east = lax.rem(s + 1, lon_size) * pieces
-            west = lax.rem(s + lon_size - 1, lon_size) * pieces + pieces - 1
-            ret[slot, s, :, width : width + LEV] = done[pl.ds(east, UNIT, stride=outer), :][:, :LEV]
-            ret[slot, s, :, padded - LEV :] = done[pl.ds(west, UNIT, stride=outer), :][
-                :, used - LEV : used
-            ]
+        def circle(m, start):
+            t, lane = divmod(start, LANES)
+
+            def tile(t):
+                index = lax.rem(m * near_tiles + t + outer, outer)
+                return done[pl.ds(index, UNIT, stride=depth), :]
+
+            if lane == 0:
+                return tile(t)
+            return jnp.concatenate([tile(t)[:, lane:], tile(t + 1)[:, :lane]], axis=1)
+
+        def gather_period(m, carry):
+            column = lax.broadcasted_iota(jnp.int32, (UNIT, LANES), 1)
+            for source in range(near_sectors):
+                target = m * near_sectors + source
+                start = source * width
+                for lane in range(0, padded, LANES):
+                    tile = circle(m, start + lane)
+                    if lane + LANES == padded:
+                        tile = jnp.where(column < LANES - LEV, tile, circle(m, start - LANES))
+                    ret[slot, target, :, lane : lane + LANES] = tile
             return carry
 
-        lax.fori_loop(0, lon_size, gather_sector, 0)
+        lax.fori_loop(0, lon_size // near_sectors, gather_period, 0)
         return_copies(slot, push)
 
     for load in table_loads:
@@ -674,8 +682,8 @@
     columns = width // LEV
     length = columns * lon_size
     nlat = row_count * lat_size
-    inner = inner_length(columns)
-    outer = length // inner
+    inner = LANES // LEV
+    depth = round_up(length // inner, 2 * SUB)
     padded = round_up(width + 2 * LEV, LANES)
     groups, turns, span, split, kept_jobs, lent_jobs = plan(lat_size, lon_size, row_count)
     slots = max(len(kept_jobs), len(lent_jobs))
@@ -686,7 +694,7 @@
     smem_spec = pl.BlockSpec(memory_space=pltpu.SMEM)
     f32 = jnp.float32
     filt = pl.pallas_call(
-        functools.partial(filter_kernel, lat_size, lon_size, inner),
+        functools.partial(filter_kernel, lat_size, lon_size),
         out_shape=jax.ShapeDtypeStruct((groups + 2, 4, UNIT, padded), f32),
         in_specs=[hbm_spec] * 3 + [smem_spec] * 2 + [hbm_spec] * TABLES,
         out_specs=vmem_spec,
@@ -694,8 +702,8 @@
         + [
             pltpu.VMEM((relays, split, span, UNIT, padded), f32),
             pltpu.VMEM((slots, lon_size, UNIT, padded), f32),
-            pltpu.VMEM((UNIT * outer, LANES), f32),
-            pltpu.VMEM((UNIT * outer, LANES), f32),
+            pltpu.VMEM((UNIT * depth, LANES), f32),
+            pltpu.VMEM((UNIT * depth, LANES), f32),
             pltpu.VMEM((slots, lon_size, UNIT, padded), f32),
             pltpu.VMEM((4, row_count, width), f32),
             pltpu.VMEM((groups + 2, 4, UNIT, padded), f32),

time: 75.5 us -> 76 us (level)
  the two profiles are of different devices: /device:TPU:7 before, /device:TPU:0 now
where the time goes in v5:
time: 76 us; the launch traced here: 75.8 us
  Pallas kernels  73.2 us (96%)
  local copies, waits for them, and re-layouts  1.96 us (3%)
    pallas_call x1, Pallas kernels, per_device(): pl.pallas_call(functools.partial(filter_kernel, lat_size, lon_size), out_...  68.8 us
    pallas_call x1, Pallas kernels, per_device(): pl.pallas_call(functools.partial(stencil_kernel, steps, lat_size, ratio),...  4.41 us
    unnamed x4, local copies, waits for them, and re-layouts  1.96 us

profile of v5, /device:TPU:0, one launch (start us, length us, event | category | flops | bytes accessed | tf_op | source)
XLA Modules:
  0.0 75.8 jit_solution(1125869825556998766)
XLA Ops:
  0.6 0.0 copy-start.1
  0.6 68.8 %polar_filter.1.below.rest_0_.rest_1_.rest_2_ = f32[18,4,4,2944]{3,2,1,0:T(4,128)} custom-call(f32[2,64,2880]{2,1,0:T(8,128)} %winds.1, f32[64,2880]{1,0:T(8,128)} %thickness.1, f32[64,2880]{1,0:T(8,128)} %tracer.1, s32[64]{0:T(128)} %cutoff.1, f32[64]{0:T(128)} %damping.1, bf16[192,576]{1,0:T(8,128)(2,1)} %constant.21.clone.rest_0_, ...), custom_call_target="tpu_custom_call" | custom-call | flops 4000000000 | bytes 6029312 | tf_op jit(solution)/shard_map/polar_filter/pallas_call | solution.py:696
  69.4 0.0 copy-done.1
  69.4 0.0 copy-start
  69.4 2.0 %copy-done = f32[18,4,4,2944]{3,2,1,0:T(4,128)S(1)} copy-done((f32[18,4,4,2944]{3,2,1,0:T(4,128)S(1)}, f32[18,4,4,2944]{3,2,1,0:T(4,128)}, u32[]{:S(2)}) %copy-start) | copy-done | bytes 3391512
  71.4 4.4 %stencil.1 = (f32[2,64,2880]{2,1,0:T(8,128)}, f32[64,2880]{1,0:T(8,128)}, f32[64,2880]{1,0:T(8,128)}) custom-call(s32[1]{0:T(128)} %bitcast.where_ref, f32[18,4,4,2944]{3,2,1,0:T(4,128)S(1)} %copy-done, f32[18,4,4,2944]{3,2,1,0:T(4,128)S(1)} %copy-done, f32[18,4,4,2944]{3,2,1,0:T(4,128)S(1)} %copy-done, f32[18,4,4,2944]{3,2,1,0:T(4,128)S(1)} %copy-done, ...), custom_call_target="tpu_custom_call" | custom-call | tf_op jit(solution)/shard_map/stencil/pallas_call | solution.py:753
Async XLA Ops:
  0.6 68.8 %copy-start.1 = (f32[256,3]{1,0:T(8,128)S(1)}, f32[256,3]{1,0:T(8,128)}, u32[]{:S(2)}) copy-start(f32[256,3]{1,0:T(8,128)} %constant.28.clone.rest_3_) | copy-start | bytes 9220
  69.4 2.0 %copy-start = (f32[18,4,4,2944]{3,2,1,0:T(4,128)S(1)}, f32[18,4,4,2944]{3,2,1,0:T(4,128)}, u32[]{:S(2)}) copy-start(f32[18,4,4,2944]{3,2,1,0:T(4,128)} %polar_filter.1.below.rest_0_.rest_1_.rest_2_) | copy-start | bytes 10174468

commit v6 on v5

--- a/solution.py
+++ b/solution.py
@@ -98,7 +98,7 @@
     jobs = []
     for field in range(0, 4, split):
         jobs += [(tuple(range(field, field + split)), turn) for turn in range(turns)]
-    lent = 3 * len(jobs) // 8 if split == 1 else len(jobs) // 2
+    lent = len(jobs) // 2
     return groups, turns, span, split, jobs[: len(jobs) - lent], jobs[len(jobs) - lent :]
 
 
@@ -561,10 +561,10 @@
             if slot + 1 < kept_count:
                 own_copies(slot, sent)
                 own_copies(slot + 1, push)
-            if slot >= 2 and slot < lent_count:
-                for copy in relay_copies(slot - 2):
+            if slot >= 1 and slot + 1 < lent_count:
+                for copy in relay_copies(slot - 1):
                     copy.wait_send()
-                for copy in relay_copies(slot):
+                for copy in relay_copies(slot + 1):
                     copy.start()
             if slot == 0 and lent_count > 1:
                 for copy in relay_copies(1):

time: 76 us -> 75.4 us (level)
  the two profiles are of different devices: /device:TPU:0 before, /device:TPU:7 now
where the time goes in v6:
time: 75.4 us; the launch traced here: 75.3 us
  Pallas kernels  72.6 us (96%)
  local copies, waits for them, and re-layouts  1.96 us (3%)
    pallas_call x1, Pallas kernels, per_device(): pl.pallas_call(functools.partial(filter_kernel, lat_size, lon_size), out_...  68.2 us
    pallas_call x1, Pallas kernels, per_device(): pl.pallas_call(functools.partial(stencil_kernel, steps, lat_size, ratio),...  4.41 us
    unnamed x4, local copies, waits for them, and re-layouts  1.96 us

profile of v6, /device:TPU:7, one launch (start us, length us, event | category | flops | bytes accessed | tf_op | source)
XLA Modules:
  0.0 75.3 jit_solution(17055821879474502138)
XLA Ops:
  0.6 0.0 copy-start.1
  0.6 68.2 %polar_filter.1.below.rest_0_.rest_1_.rest_2_ = f32[18,4,4,2944]{3,2,1,0:T(4,128)} custom-call(f32[2,64,2880]{2,1,0:T(8,128)} %winds.1, f32[64,2880]{1,0:T(8,128)} %thickness.1, f32[64,2880]{1,0:T(8,128)} %tracer.1, s32[64]{0:T(128)} %cutoff.1, f32[64]{0:T(128)} %damping.1, bf16[192,576]{1,0:T(8,128)(2,1)} %constant.21.clone.rest_0_, ...), custom_call_target="tpu_custom_call" | custom-call | flops 4000000000 | bytes 6029312 | tf_op jit(solution)/shard_map/polar_filter/pallas_call | solution.py:696
  68.9 0.0 copy-done.1
  68.9 0.0 copy-start
  68.9 2.0 %copy-done = f32[18,4,4,2944]{3,2,1,0:T(4,128)S(1)} copy-done((f32[18,4,4,2944]{3,2,1,0:T(4,128)S(1)}, f32[18,4,4,2944]{3,2,1,0:T(4,128)}, u32[]{:S(2)}) %copy-start) | copy-done | bytes 3391512
  70.9 4.4 %stencil.1 = (f32[2,64,2880]{2,1,0:T(8,128)}, f32[64,2880]{1,0:T(8,128)}, f32[64,2880]{1,0:T(8,128)}) custom-call(s32[1]{0:T(128)} %bitcast.where_ref, f32[18,4,4,2944]{3,2,1,0:T(4,128)S(1)} %copy-done, f32[18,4,4,2944]{3,2,1,0:T(4,128)S(1)} %copy-done, f32[18,4,4,2944]{3,2,1,0:T(4,128)S(1)} %copy-done, f32[18,4,4,2944]{3,2,1,0:T(4,128)S(1)} %copy-done, ...), custom_call_target="tpu_custom_call" | custom-call | tf_op jit(solution)/shard_map/stencil/pallas_call | solution.py:753
Async XLA Ops:
  0.6 68.3 %copy-start.1 = (f32[256,3]{1,0:T(8,128)S(1)}, f32[256,3]{1,0:T(8,128)}, u32[]{:S(2)}) copy-start(f32[256,3]{1,0:T(8,128)} %constant.28.clone.rest_3_) | copy-start | bytes 9220
  68.9 2.0 %copy-start = (f32[18,4,4,2944]{3,2,1,0:T(4,128)S(1)}, f32[18,4,4,2944]{3,2,1,0:T(4,128)}, u32[]{:S(2)}) copy-start(f32[18,4,4,2944]{3,2,1,0:T(4,128)} %polar_filter.1.below.rest_0_.rest_1_.rest_2_) | copy-start | bytes 10174468
